TPU v7x, 128 devices: a whole 4x4x4 slice. The times are simulated.
128 devices in a mesh: tensor: 8 (over z_lo, y), dp: 16 (over x, z_hi, core).
Axes of the slice: x: 4, y: 4, z: 4 (z_hi: 2, z_lo: 2; z = z_hi * 2 + z_lo), core: 2. Of those that a mesh axis runs over, the one named last changes fastest.
Arguments:
- tokens: bfloat16 [2048, 1024], P('dp'), may hold values from -6 to 6
- segment_ids: int32 [2048], replicated, may hold values from 0 to 2, as said below
- norm_gain: bfloat16 [2, 2, 1024], replicated, may hold values from 0.25 to 1.75
- norm_bias: bfloat16 [2, 2, 1024], replicated, may hold values from -1.5 to 1.5
- w_qkv: bfloat16 [2, 1024, 3, 1024], P(None, None, None, 'tensor'), may hold values from -0.1875 to 0.1875
- b_qv: bfloat16 [2, 2, 1024], P(None, None, 'tensor'), may hold values from -1.5 to 1.5
- w_out: bfloat16 [2, 1024, 1024], P(None, 'tensor'), may hold values from -2 to 2
- b_out: bfloat16 [2, 1024], replicated, may hold values from -1.5 to 1.5
- w_fc: bfloat16 [2, 1024, 4096], P(None, None, 'tensor'), may hold values from -0.1875 to 0.1875
- b_fc: bfloat16 [2, 4096], P(None, 'tensor'), may hold values from -2.5 to 2.5
- w_proj: bfloat16 [2, 4096, 1024], P(None, 'tensor'), may hold values from -0.09375 to 0.09375
- b_proj: bfloat16 [2, 1024], replicated, may hold values from -1.5 to 1.5
- cotangent: bfloat16 [2048, 1024], P('dp'), may hold values from -6 to 6
Outputs:
- out: float32 [2048, 1024], P('dp')
- grad_input: float32 [2048, 1024], P('dp')
- g_norm_gain: float32 [2, 2, 1024], replicated
- g_norm_bias: float32 [2, 2, 1024], replicated
- g_w_qkv: float32 [2, 1024, 3, 1024], P(None, None, None, 'tensor')
- g_b_qv: float32 [2, 2, 1024], P(None, None, 'tensor')
- g_w_out: float32 [2, 1024, 1024], P(None, 'tensor')
- g_b_out: float32 [2, 1024], replicated
- g_w_fc: float32 [2, 1024, 4096], P(None, None, 'tensor')
- g_b_fc: float32 [2, 4096], P(None, 'tensor')
- g_w_proj: float32 [2, 4096, 1024], P(None, 'tensor')
- g_b_proj: float32 [2, 1024], replicated
Inputs may be any that keep to these rules, and one draw needn't show every extreme that they name: `segment_ids`: never falling along the tokens; segment 1 holds token 127 and token 1920; segments 0 and 2 each hold 1 to 127 tokens.
All inputs are finite; a program needn't handle non-finite values.
Results may differ from a plain program's by a relative error of at most 0.023.
Values may be sent and summed in bfloat16 or wider, within the bound.
No kernel may reach another device: no remote copies, remote signals or barrier semaphores. Data moves between devices by JAX's collectives and lax.ppermute only.
A program may use at most 128 MiB of HBM per device.

v0:
```python
import functools

import jax
import jax.numpy as jnp
from jax import lax
from jax.experimental import pallas as pl
from jax.experimental.pallas import tpu as pltpu
from jax.sharding import PartitionSpec as P

HD = 64
F32 = jnp.float32
BF16 = jnp.bfloat16
ROOT = 0.7978845608028654
CUBE = 0.044715


def dot(left, right):
    return jnp.dot(left, right, preferred_element_type=F32)


def dot_t(left, right):
    return lax.dot_general(left, right, (((1,), (1,)), ((), ())), preferred_element_type=F32)


def norm_parts(value):
    mean = jnp.mean(value, -1, keepdims=True)
    centered = value - mean
    spread = jnp.mean(centered * centered, -1, keepdims=True)
    factor = lax.rsqrt(spread + 1e-05)
    return centered * factor, factor


def tanh_part(value):
    return jnp.tanh(ROOT * (value + CUBE * value * value * value))


def gelu(value):
    return 0.5 * value * (1.0 + tanh_part(value))


def gelu_slope(value):
    bend = tanh_part(value)
    inner = ROOT * (1.0 + 3.0 * CUBE * value * value)
    return 0.5 * (1.0 + bend) + 0.5 * value * (1.0 - bend * bend) * inner


def call(kernel, outs, layered, *args):
    layer, wide = layered

    def spec(index, arg):
        if arg.dtype == jnp.int32 and arg.shape == (1,):
            return pl.BlockSpec(memory_space=pltpu.SMEM)
        if index in wide:
            rest = arg.shape[1:]
            return pl.BlockSpec((None,) + rest, lambda i: (layer,) + (0,) * len(rest))
        return pl.BlockSpec(arg.shape, lambda i: (0,) * arg.ndim)

    return pl.pallas_call(
        kernel,
        grid=(1,),
        in_specs=[spec(index, arg) for index, arg in enumerate(args)],
        out_specs=[pl.BlockSpec(out.shape, lambda i, n=len(out.shape): (0,) * n) for out in outs],
        out_shape=outs,
        compiler_params=pltpu.CompilerParams(vmem_limit_bytes=40 * 1024 * 1024),
    )(*args)


def shape(dims, kind):
    return jax.ShapeDtypeStruct(dims, kind)


def project(a_low, w_ref, bias_ref, q_ref, kv_ref, all_ref):
    q_ref[...] = (dot(a_low, w_ref[0]) + bias_ref[0:1].astype(F32)).astype(BF16)
    k_low = dot(a_low, w_ref[1]).astype(BF16)
    v_low = (dot(a_low, w_ref[2]) + bias_ref[1:2].astype(F32)).astype(BF16)
    local = k_low.shape[1]
    kv_ref[:, :local] = k_low
    kv_ref[:, local:] = v_low
    for index in range(all_ref.shape[0]):
        all_ref[index, :, :local] = k_low
        all_ref[index, :, local:] = v_low


def first_kernel(x_ref, gain_ref, shift_ref, w_ref, bias_ref, a_ref, q_ref, kv_ref, all_ref):
    normed, _ = norm_parts(x_ref[...].astype(F32))
    a_low = (normed * gain_ref[...] + shift_ref[...]).astype(BF16)
    a_ref[...] = a_low
    project(a_low, w_ref, bias_ref, q_ref, kv_ref, all_ref)


def project_kernel(a_ref, w_ref, bias_ref, q_ref, kv_ref, all_ref):
    project(a_ref[...], w_ref, bias_ref, q_ref, kv_ref, all_ref)


def head_masks(rows, local):
    column = lax.broadcasted_iota(jnp.int32, (rows, local), 1)
    return [column < HD, column >= HD]


def only(mask, value):
    return jnp.where(mask, value.astype(F32), 0.0).astype(BF16)


def allowed_of(start_ref, own_ref, all_ref, own_is_query):
    own_spot = start_ref[0] + lax.broadcasted_iota(jnp.int32, own_ref.shape, 0)
    spots = lax.broadcasted_iota(jnp.int32, all_ref.shape, 1)
    order = spots <= own_spot if own_is_query else spots >= own_spot
    return (all_ref[...] == own_ref[...]) & order


def attend_kernel(start_ref, own_ref, all_ref, q_ref, kv_ref, w_ref, o_ref, low_ref, log_ref, part_ref):
    rows, local = q_ref.shape
    total = all_ref.shape[1]
    keys = kv_ref[:, :, :local].reshape(total, local)
    values = kv_ref[:, :, local:].reshape(total, local)
    allowed = allowed_of(start_ref, own_ref, all_ref, True)
    queries = q_ref[...].astype(F32) * HD ** (-0.5)
    masks = head_masks(rows, local)
    outs, logs = [], []
    for mask in masks:
        scores = jnp.where(allowed, dot_t(only(mask, queries), keys), -1e30)
        top = jnp.max(scores, -1, keepdims=True)
        expd = jnp.exp(scores - top)
        denom = jnp.sum(expd, -1, keepdims=True)
        outs.append(dot((expd * (1.0 / denom)).astype(BF16), values))
        logs.append(top + jnp.log(denom))
    attended = jnp.where(masks[0], outs[0], outs[1])
    o_low = attended.astype(BF16)
    o_ref[...] = attended
    low_ref[...] = o_low
    log_ref[...] = jnp.where(masks[0], logs[0], logs[1])
    part_ref[...] = dot(o_low, w_ref[...]).astype(BF16).reshape(part_ref.shape)


def sum_parts(ref, start, rows):
    total = ref[0, start : start + rows].astype(F32)
    for index in range(1, ref.shape[0]):
        total = total + ref[index, start : start + rows].astype(F32)
    return total


def row_kernel(parts_ref, state_ref, bias_ref, gain_ref, shift_ref, state_out, normed_ref, factor_ref, sent_ref):
    state = state_ref[...] + (sum_parts(parts_ref, 0, state_ref.shape[0]) + bias_ref[...])
    normed, factor = norm_parts(state)
    low = (normed * gain_ref[...] + shift_ref[...]).astype(BF16)
    state_out[...] = state
    normed_ref[...] = normed
    factor_ref[...] = jnp.broadcast_to(factor, factor_ref.shape)
    for index in range(sent_ref.shape[0]):
        sent_ref[index] = low


def forward_kernel(b_ref, fc_ref, bias_ref, proj_ref, pre_ref, h_ref, part_ref):
    pre = dot(b_ref[...], fc_ref[...]) + bias_ref[...].astype(F32)
    h_low = gelu(pre).astype(BF16)
    pre_ref[...] = pre
    h_ref[...] = h_low
    part_ref[...] = dot(h_low, proj_ref[...]).astype(BF16).reshape(part_ref.shape)


def turn_kernel(b_ref, fc_ref, bias_ref, proj_ref, g_ref, h_ref, gf_ref, part_ref):
    share = part_ref.shape[1] // 2
    pre = dot(b_ref[...], fc_ref[...]) + bias_ref[...].astype(F32)
    h_low = gelu(pre).astype(BF16)
    h_ref[...] = h_low
    parts = dot(h_low, proj_ref[...]).astype(BF16)
    part_ref[:, :share] = parts.reshape(-1, share, parts.shape[1])
    g_f = (dot_t(g_ref[...], proj_ref[...]) * gelu_slope(pre)).astype(BF16)
    gf_ref[...] = g_f
    parts = dot_t(g_f, fc_ref[...]).astype(BF16)
    part_ref[:, share:] = parts.reshape(-1, share, parts.shape[1])


def backward_kernel(g_ref, pre_ref, fc_ref, proj_ref, gf_ref, part_ref):
    g_f = (dot_t(g_ref[...], proj_ref[...]) * gelu_slope(pre_ref[...])).astype(BF16)
    gf_ref[...] = g_f
    part_ref[...] = dot_t(g_f, fc_ref[...]).astype(BF16).reshape(part_ref.shape)


def norm_back(d_value, normed_ref, factor_ref, gain_ref, grad_ref, sums_ref):
    normed = normed_ref[...]
    scaled = d_value * gain_ref[...]
    back = factor_ref[:, 0:1] * (
        scaled
        - jnp.mean(scaled, -1, keepdims=True)
        - normed * jnp.mean(scaled * normed, -1, keepdims=True)
    )
    sums_ref[0:1] = jnp.sum(d_value * normed, 0, keepdims=True)
    sums_ref[1:2] = jnp.sum(d_value, 0, keepdims=True)
    return grad_ref[...] + back


def back_kernel(parts_ref, normed_ref, factor_ref, gain_ref, grad_ref, grad_out, sums_ref, sent_ref):
    share = normed_ref.shape[0]
    grad = norm_back(sum_parts(parts_ref, 0, share), normed_ref, factor_ref, gain_ref, grad_ref, sums_ref)
    grad_out[...] = grad
    low = grad.astype(BF16)
    for index in range(sent_ref.shape[0]):
        sent_ref[index] = low


def turn_back_kernel(
    parts_ref, state_ref, bias_ref, normed_ref, factor_ref, gain_ref, grad_ref, grad_out, sums_ref, sent_ref
):
    share = normed_ref.shape[0]
    out = (state_ref[...] + (sum_parts(parts_ref, 0, share) + bias_ref[...])).astype(BF16)
    grad = norm_back(sum_parts(parts_ref, share, share), normed_ref, factor_ref, gain_ref, grad_ref, sums_ref)
    grad_out[...] = grad
    low = grad.astype(BF16)
    for index in range(sent_ref.shape[0]):
        sent_ref[index, :share] = low
        sent_ref[index, share:] = out


def two_terms(value):
    high = value.astype(BF16).astype(F32)
    return high, value - high


def output_back_kernel(gy_ref, w_ref, o_ref, log_ref, go_ref, delta_ref, sent_ref):
    rows, local = o_ref.shape
    g_o = dot_t(gy_ref[...], w_ref[...]).astype(BF16)
    go_ref[...] = g_o
    masks = head_masks(rows, local)
    product = g_o.astype(F32) * o_ref[...]
    deltas = [jnp.sum(jnp.where(mask, product, 0.0), -1, keepdims=True) for mask in masks]
    delta = jnp.where(masks[0], deltas[0], deltas[1])
    delta_ref[...] = delta
    rows_of = []
    for value in (log_ref[...], delta):
        turned = value.T
        high, rest = two_terms(jnp.concatenate((turned[0:1], turned[HD : HD + 1]), 0))
        rows_of += [high, rest]
    rows_of.append(jnp.zeros((8, local), F32))
    extra = jnp.concatenate(rows_of, 0).astype(BF16)
    for index in range(sent_ref.shape[0]):
        sent_ref[index, :rows] = g_o
        sent_ref[index, rows:] = extra


def query_back_kernel(start_ref, own_ref, all_ref, q_ref, kv_ref, go_ref, log_ref, delta_ref, gq_ref):
    rows, local = q_ref.shape
    total = all_ref.shape[1]
    keys = kv_ref[:, :, :local].reshape(total, local)
    values = kv_ref[:, :, local:].reshape(total, local)
    allowed = allowed_of(start_ref, own_ref, all_ref, True)
    queries = q_ref[...].astype(F32) * HD ** (-0.5)
    masks = head_masks(rows, local)
    outs = []
    for head, mask in enumerate(masks):
        at = slice(head * HD, head * HD + 1)
        scores = jnp.where(allowed, dot_t(only(mask, queries), keys), -1e30)
        probs = jnp.exp(scores - log_ref[:, at])
        d_probs = dot_t(only(mask, go_ref[...]), values)
        g_s = (probs * (d_probs - delta_ref[:, at])).astype(BF16)
        outs.append(dot(g_s, keys))
    gq_ref[...] = (jnp.where(masks[0], outs[0], outs[1]) * HD ** (-0.5)).astype(BF16)


def key_back_kernel(start_ref, own_ref, all_ref, kv_ref, q_ref, got_ref, gq_ref, w_ref, gkv_ref, part_ref):
    rows, twice = kv_ref.shape
    local = twice // 2
    total = all_ref.shape[1]
    allowed = allowed_of(start_ref, own_ref, all_ref, False)
    queries = q_ref[...]
    g_o = got_ref[:, :rows].reshape(total, local)
    extra = got_ref[:, rows:].astype(F32)
    keys = kv_ref[:, :local].astype(F32) * HD ** (-0.5)
    values = kv_ref[:, local:]
    masks = head_masks(rows, local)
    d_keys, d_values = [], []
    for head, mask in enumerate(masks):

        def row_of(base):
            row = extra[:, base + head : base + head + 1] + extra[:, base + 2 + head : base + 3 + head]
            return jnp.concatenate([row[index] for index in range(row.shape[0])], 1)

        scores = jnp.where(allowed, dot_t(only(mask, keys), queries), -1e30)
        probs = jnp.exp(scores - row_of(0))
        d_probs = dot_t(only(mask, values), g_o)
        g_s = (probs * (d_probs - row_of(4))).astype(BF16)
        d_keys.append(dot(g_s, queries))
        d_values.append(dot(probs.astype(BF16), g_o))
    g_k = (jnp.where(masks[0], d_keys[0], d_keys[1]) * HD ** (-0.5)).astype(BF16)
    g_v = jnp.where(masks[0], d_values[0], d_values[1]).astype(BF16)
    gkv_ref[:, :local] = g_k
    gkv_ref[:, local:] = g_v
    part = dot_t(gq_ref[...], w_ref[0]) + dot_t(g_k, w_ref[1]) + dot_t(g_v, w_ref[2])
    part_ref[...] = part.astype(BF16).reshape(part_ref.shape)


def swap_all(value, axis):
    return lax.all_to_all(value, axis, 0, 0)


def column_sum(value):
    return jnp.sum(value.astype(F32), 0)


def cross(left, right):
    return lax.dot_general(left, right, (((0,), (0,)), ((), ())), preferred_element_type=F32)


def pair_sums(parts, turn, after):
    place = lax.axis_index("dp")
    count = lax.axis_size("dp")
    x_low, x_high = (place // 4) % 2, place // 8
    along_x = ((x_low ^ x_high, 4), (x_high, 12)) if turn else ((x_high, 12), (x_low ^ x_high, 4))
    steps = ((place % 2, 1),) + along_x + (((place // 2) % 2, 2),)

    def swap(value, flip):
        return lax.ppermute(value, "dp", [(i, i ^ flip) for i in range(count)])

    for bit, flip in steps:
        halves = parts.reshape((2, -1) + parts.shape[1:])
        mine = lax.dynamic_index_in_dim(halves, bit, 0, keepdims=False)
        other = lax.dynamic_index_in_dim(halves, 1 - bit, 0, keepdims=False)
        parts = (mine.astype(F32) + swap(other, flip).astype(F32)).astype(BF16)
    parts = lax.optimization_barrier((parts, after))[0]
    for bit, flip in reversed(steps):
        got = swap(parts, flip)
        parts = jnp.concatenate((jnp.where(bit, got, parts), jnp.where(bit, parts, got)), 0)
    return parts


def body(
    tokens,
    segment_ids,
    norm_gain,
    norm_bias,
    w_qkv,
    b_qv,
    w_out,
    b_out,
    w_fc,
    b_fc,
    w_proj,
    b_proj,
    cotangent,
):
    rows, width = tokens.shape
    total = segment_ids.shape[0]
    layers = w_qkv.shape[0]
    local = w_qkv.shape[3]
    hidden = w_fc.shape[2]
    ranks, slots = lax.axis_size("dp"), lax.axis_size("tensor")
    share = rows // slots
    first = (lax.axis_index("dp") * rows).astype(jnp.int32)
    own = lax.axis_index("tensor") * share
    start = first.reshape(1)
    seg_own = lax.dynamic_slice_in_dim(segment_ids, first, rows).reshape(rows, 1)
    seg_all = segment_ids.reshape(1, total)
    spots = (start, seg_own, seg_all)
    gains = norm_gain.astype(F32).reshape(layers, 2, 1, width)
    shifts = norm_bias.astype(F32).reshape(layers, 2, 1, width)
    out_bias = b_out.astype(F32).reshape(layers, 1, width)
    end_bias = b_proj.astype(F32).reshape(layers, 1, width)
    w_three = w_qkv.transpose(0, 2, 1, 3)
    fc_bias = b_fc.reshape(layers, 1, hidden)
    state = lax.dynamic_slice_in_dim(tokens, own, share).astype(F32)
    a_normed, a_factor = norm_parts(state)
    a_factor = jnp.broadcast_to(a_factor, (share, 128))
    row_block = shape((share, width), F32)
    row_stat = shape((share, 128), F32)
    exchange = shape((slots, share, width), BF16)
    saved = []
    qkv_shapes = [
        shape((rows, local), BF16),
        shape((rows, 2 * local), BF16),
        shape((ranks, rows, 2 * local), BF16),
    ]
    a_low = None
    for layer in range(layers):
        if layer:
            q_low, kv_own, kv_sent = call(project_kernel, qkv_shapes, (layer, (1, 2)), a_low, w_three, b_qv)
        else:
            a_low, q_low, kv_own, kv_sent = call(
                first_kernel,
                [shape((rows, width), BF16)] + qkv_shapes,
                (layer, (3, 4)),
                tokens,
                gains[0, 0],
                shifts[0, 0],
                w_three,
                b_qv,
            )
        kv_all = swap_all(kv_sent, "dp")
        o_full, o_low, logs, attn_parts = call(
            attend_kernel,
            [shape((rows, local), F32), shape((rows, local), BF16), shape((rows, local), F32), exchange],
            (layer, (5,)),
            *spots,
            q_low,
            kv_all,
            w_out,
        )
        middle, b_normed, b_factor, b_sent = call(
            row_kernel,
            [row_block, row_block, row_stat, exchange],
            (layer, ()),
            swap_all(attn_parts, "tensor"),
            state,
            out_bias[layer],
            gains[layer, 1],
            shifts[layer, 1],
        )
        b_low = swap_all(b_sent, "tensor").reshape(rows, width)
        kept = [a_normed, a_factor, a_low, q_low, kv_own, kv_all, o_full, o_low, logs, b_normed, b_factor, b_low]
        if layer < layers - 1:
            pre, h_low, parts = call(
                forward_kernel,
                [shape((rows, hidden), F32), shape((rows, hidden), BF16), exchange],
                (layer, (1, 2, 3)),
                b_low,
                w_fc,
                fc_bias,
                w_proj,
            )
            state, a_normed, a_factor, a_sent = call(
                row_kernel,
                [row_block, row_block, row_stat, exchange],
                (layer, ()),
                swap_all(parts, "tensor"),
                middle,
                end_bias[layer],
                gains[layer + 1, 0],
                shifts[layer + 1, 0],
            )
            a_low = swap_all(a_sent, "tensor").reshape(rows, width)
            kept += [pre, h_low]
        saved.append(kept)
    q_every = lax.all_gather(jnp.concatenate([kept[3] for kept in saved], 1), "dp", axis=0, tiled=True)
    g_m = cotangent
    grad = lax.dynamic_slice_in_dim(cotangent, own, share).astype(F32)
    done = [None] * layers
    smalls, sums = [], []
    two_rows = shape((2, width), F32)
    out = None
    for layer in reversed(range(layers)):
        a_normed, a_factor, a_low, q_low, kv_own, kv_all, o_full, o_low, logs, b_normed, b_factor, b_low = (
            saved[layer][:12]
        )
        if layer == layers - 1:
            double = shape((slots, 2 * share, width), BF16)
            h_low, g_f, parts = call(
                turn_kernel,
                [shape((rows, hidden), BF16), shape((rows, hidden), BF16), double],
                (layer, (1, 2, 3)),
                b_low,
                w_fc,
                fc_bias,
                w_proj,
                g_m,
            )
            grad, sums_b, sent = call(
                turn_back_kernel,
                [row_block, two_rows, double],
                (layer, ()),
                swap_all(parts, "tensor"),
                middle,
                end_bias[layer],
                b_normed,
                b_factor,
                gains[layer, 1],
                grad,
            )
            got = swap_all(sent, "tensor")
            g_y = got[:, :share].reshape(rows, width)
            out = got[:, share:].reshape(rows, width).astype(F32)
        else:
            pre, h_low = saved[layer][12:]
            g_f, parts = call(
                backward_kernel,
                [shape((rows, hidden), BF16), exchange],
                (layer, (2, 3)),
                g_m,
                pre,
                w_fc,
                w_proj,
            )
            grad, sums_b, sent = call(
                back_kernel,
                [row_block, two_rows, exchange],
                (layer, ()),
                swap_all(parts, "tensor"),
                b_normed,
                b_factor,
                gains[layer, 1],
                grad,
            )
            g_y = swap_all(sent, "tensor").reshape(rows, width)
        g_o, delta, sent = call(
            output_back_kernel,
            [shape((rows, local), BF16), shape((rows, local), F32), shape((ranks, rows + 16, local), BF16)],
            (layer, (1,)),
            g_y,
            w_out,
            o_full,
            logs,
        )
        go_all = swap_all(sent, "dp")
        (g_q,) = call(
            query_back_kernel,
            [shape((rows, local), BF16)],
            (layer, ()),
            *spots,
            q_low,
            kv_all,
            g_o,
            logs,
            delta,
        )
        g_kv, parts = call(
            key_back_kernel,
            [shape((rows, 2 * local), BF16), exchange],
            (layer, (7,)),
            *spots,
            kv_own,
            q_every[:, layer * local : (layer + 1) * local],
            go_all,
            g_q,
            w_three,
        )
        grad, sums_a, sent = call(
            back_kernel,
            [row_block, two_rows, exchange],
            (layer, ()),
            swap_all(parts, "tensor"),
            a_normed,
            a_factor,
            gains[layer, 0],
            grad,
        )
        sums = [sums_a, sums_b] + sums
        smalls = [
            column_sum(g_y),
            column_sum(g_m),
            column_sum(g_q),
            column_sum(g_kv[:, local:]),
            column_sum(g_f),
        ] + smalls
        g_w_qkv = cross(a_low, jnp.concatenate((g_q, g_kv), 1))
        big = tuple(
            part.astype(BF16) for part in (cross(h_low, g_m), cross(b_low, g_f), cross(o_low, g_y), g_w_qkv)
        )
        if layer:
            g_m = swap_all(sent, "tensor").reshape(rows, width)
            done[layer] = lax.psum(big, "dp")
    early = tuple(
        pair_sums(part.reshape(ranks, -1, part.shape[1]), turn, g_kv).reshape(part.shape)
        for turn, part in enumerate(big[:2])
    )
    tail = jnp.concatenate([sent, jnp.broadcast_to(jnp.concatenate(sums, 0).astype(BF16), (slots, 8, width))], 1)
    got = swap_all(tail, "tensor")
    grad_input = got[:, :share].reshape(rows, width).astype(F32)
    norm_sums = jnp.sum(got[:, share:].astype(F32), 0)
    small = jnp.concatenate([norm_sums.reshape(-1)] + smalls)
    each = small.size // (8 * ranks)
    wide = 4 * width
    packed = jnp.concatenate(
        (
            big[2].reshape(ranks, 8, width),
            big[3].reshape(ranks, 8, 8, 3 * local).transpose(0, 2, 1, 3).reshape(ranks, 8, 3 * width),
            jnp.pad(small.astype(BF16).reshape(ranks, 8, each), ((0, 0), (0, 0), (0, 128 - each))),
        ),
        2,
    )
    mine = jnp.sum(swap_all(packed, "dp").astype(F32), 0).astype(BF16)
    got = swap_all(jnp.broadcast_to(mine, (ranks,) + mine.shape), "dp")
    late_out = got[:, :, :width].reshape(big[2].shape)
    late_qkv = got[:, :, width:wide].reshape(ranks, 8, 8, 3 * local).transpose(0, 2, 1, 3).reshape(big[3].shape)
    done[0] = early + (late_out, late_qkv)
    small = got[:, :, wide : wide + each].reshape(-1).astype(F32)
    norm_grads = small[: 8 * width].reshape(layers, 2, 2, width)
    per_layer = small[8 * width :].reshape(layers, -1)
    cut = 2 * width

    def both(index):
        return jnp.stack([done[layer][index] for layer in range(layers)]).astype(F32)

    return (
        out,
        grad_input,
        norm_grads[:, :, 0],
        norm_grads[:, :, 1],
        both(3).reshape(layers, width, 3, local),
        per_layer[:, cut : cut + 2 * local].reshape(layers, 2, local),
        both(2),
        per_layer[:, :width],
        both(1),
        per_layer[:, cut + 2 * local :],
        both(0),
        per_layer[:, width:cut],
    )


def solution(mesh):
    in_specs = (
        P("dp", None),
        P(),
        P(),
        P(),
        P(None, None, None, "tensor"),
        P(None, None, "tensor"),
        P(None, "tensor", None),
        P(),
        P(None, None, "tensor"),
        P(None, "tensor"),
        P(None, "tensor", None),
        P(),
        P("dp", None),
    )
    out_specs = (
        P("dp", None),
        P("dp", None),
        P(),
        P(),
        P(None, None, None, "tensor"),
        P(None, None, "tensor"),
        P(None, "tensor", None),
        P(),
        P(None, None, "tensor"),
        P(None, "tensor"),
        P(None, "tensor", None),
        P(),
    )
    return jax.shard_map(body, mesh=mesh, in_specs=in_specs, out_specs=out_specs, check_vma=False)
```

profile of v0, /device:TPU:1, one launch (start us, length us, event | category | flops | bytes accessed | tf_op | source)
XLA Modules:
  0.0 466.7 jit_solution(6085035057487897103)
XLA Ops:
  14.6 9.3 %all-to-all-start = ((bf16[16,128,256]{2,1,0:T(8,128)(2,1)}), bf16[16,128,256]{2,1,0:T(8,128)(2,1)S(1)}, u32[]{:S(2)}, u32[]{:S(2)}) async-start(bf16[16,128,256]{2,1,0:T(8,128)(2,1)} %copy-done.15), calls=%async_computation | async-start | bytes 2097152 | tf_op jit(solution)/shard_map/all_to_all | solution.py:293
  24.1 17.0 %all-to-all-done.kv_ref = bf16[16,128,256]{2,1,0:T(8,128)(2,1)S(1)} async-done(((bf16[16,128,256]{2,1,0:T(8,128)(2,1)}), bf16[16,128,256]{2,1,0:T(8,128)(2,1)S(1)}, u32[]{:S(2)}, u32[]{:S(2)}) %all-to-all-start) | async-done | bytes 1048608 | tf_op jit(solution)/shard_map/all_to_all | solution.py:293
  41.1 2.6 shard_map.221
  43.7 4.7 all-to-all-start.1
  49.8 5.1 %all-to-all-done.1.parts_ref = bf16[8,16,1024]{2,1,0:T(8,128)(2,1)S(1)} async-done(((bf16[8,16,1024]{2,1,0:T(8,128)(2,1)}), bf16[8,16,1024]{2,1,0:T(8,128)(2,1)S(1)}, u32[]{:S(2)}, u32[]{:S(2)}) %all-to-all-start.1) | async-done | bytes 262176 | tf_op jit(solution)/shard_map/all_to_all | solution.py:293
  55.8 3.4 all-to-all-start.2
  59.3 6.0 %all-to-all-done.2 = bf16[8,16,1024]{2,1,0:T(8,128)(2,1)S(1)} async-done(((bf16[8,16,1024]{2,1,0:T(8,128)(2,1)}), bf16[8,16,1024]{2,1,0:T(8,128)(2,1)S(1)}, u32[]{:S(2)}, u32[]{:S(2)}) %all-to-all-start.2) | async-done | bytes 262176 | tf_op jit(solution)/shard_map/all_to_all | solution.py:293
  71.3 3.4 all-to-all-start.3
  75.3 5.5 %all-to-all-done.3.parts_ref = bf16[8,16,1024]{2,1,0:T(8,128)(2,1)S(1)} async-done(((bf16[8,16,1024]{2,1,0:T(8,128)(2,1)}), bf16[8,16,1024]{2,1,0:T(8,128)(2,1)S(1)}, u32[]{:S(2)}, u32[]{:S(2)}) %all-to-all-start.3) | async-done | bytes 262176 | tf_op jit(solution)/shard_map/all_to_all | solution.py:293
  81.9 8.5 %all_to_all.100 = bf16[8,16,1024]{2,1,0:T(8,128)(2,1)S(1)} all-to-all(bf16[8,16,1024]{2,1,0:T(8,128)(2,1)S(1)} %get-tuple-element.76), channel_id=1, replica_groups=mesh['tensor'=8,'dp'=16] {'tensor'}, dimensions={0} | all-to-all | bytes 524288 | tf_op jit(solution)/shard_map/all_to_all | solution.py:293
  94.0 9.9 %all-to-all-start.5 = ((bf16[16,128,256]{2,1,0:T(8,128)(2,1)}), bf16[16,128,256]{2,1,0:T(8,128)(2,1)}, u32[]{:S(2)}, u32[]{:S(2)}) async-start(bf16[16,128,256]{2,1,0:T(8,128)(2,1)} %copy-done.16), calls=%async_computation.5 | async-start | bytes 2097152 | tf_op jit(solution)/shard_map/all_to_all | solution.py:293
  104.6 16.6 %all-to-all-done.5.kv_ref = bf16[16,128,256]{2,1,0:T(8,128)(2,1)} async-done(((bf16[16,128,256]{2,1,0:T(8,128)(2,1)}), bf16[16,128,256]{2,1,0:T(8,128)(2,1)}, u32[]{:S(2)}, u32[]{:S(2)}) %all-to-all-start.5) | async-done | bytes 1048608 | tf_op jit(solution)/shard_map/all_to_all | solution.py:293
  121.2 3.2 shard_map.226
  124.4 8.7 %all_to_all.101.parts_ref = bf16[8,16,1024]{2,1,0:T(8,128)(2,1)S(1)} all-to-all(bf16[8,16,1024]{2,1,0:T(8,128)(2,1)S(1)} %get-tuple-element.79), channel_id=1, replica_groups=mesh['tensor'=8,'dp'=16] {'tensor'}, dimensions={0} | all-to-all | bytes 524288 | tf_op jit(solution)/shard_map/all_to_all | solution.py:293
  135.3 4.0 all-to-all-start.7
  140.3 5.3 %all-to-all-done.7 = bf16[8,16,1024]{2,1,0:T(8,128)(2,1)} async-done(((bf16[8,16,1024]{2,1,0:T(8,128)(2,1)}), bf16[8,16,1024]{2,1,0:T(8,128)(2,1)}, u32[]{:S(2)}, u32[]{:S(2)}) %all-to-all-start.7) | async-done | bytes 262176 | tf_op jit(solution)/shard_map/all_to_all | solution.py:293
  153.8 4.1 all-to-all-start.8
  160.3 5.3 %all-to-all-done.8.parts_ref = bf16[8,32,1024]{2,1,0:T(8,128)(2,1)} async-done(((bf16[8,32,1024]{2,1,0:T(8,128)(2,1)}), bf16[8,32,1024]{2,1,0:T(8,128)(2,1)}, u32[]{:S(2)}, u32[]{:S(2)}) %all-to-all-start.8) | async-done | bytes 524320 | tf_op jit(solution)/shard_map/all_to_all | solution.py:293
  170.7 4.1 all-to-all-start.9
  189.1 9.0 %all-to-all-start.10 = ((bf16[16,144,128]{2,1,0:T(8,128)(2,1)}), bf16[16,144,128]{2,1,0:T(8,128)(2,1)}, u32[]{:S(2)}, u32[]{:S(2)}) async-start(bf16[16,144,128]{2,1,0:T(8,128)(2,1)} %copy-done.19), calls=%async_computation.10 | async-start | bytes 1179648 | tf_op jit(solution)/shard_map/all_to_all | solution.py:293
  201.9 2.5 shard_map.231.gq_ref
  206.7 3.1 all-to-all-done.10.got_ref
  211.7 2.8 shard_map.232
  215.9 4.6 all-to-all-start.11
  222.3 4.3 all-to-all-done.11.parts_ref
  231.7 3.4 all-to-all-start.12
  237.4 3.8 all-to-all-done.12
  247.7 4.0 all-to-all-start.13
  255.1 4.1 collective-permute-start
  264.8 5.3 %all-to-all-start.14 = ((bf16[8,16,1024]{2,1,0:T(8,128)(2,1)}), bf16[8,16,1024]{2,1,0:T(8,128)(2,1)S(1)}, u32[]{:S(2)}, u32[]{:S(2)}) async-start(bf16[8,16,1024]{2,1,0:T(8,128)(2,1)} %copy-done.36), calls=%async_computation.14 | async-start | bytes 524288 | tf_op jit(solution)/shard_map/all_to_all | solution.py:293
  285.4 3.6 all-to-all-start.15
  297.5 8.2 %collective-permute-done.1 = bf16[4,64,512]{2,1,0:T(8,128)(2,1)S(1)} collective-permute-done((bf16[4,64,512]{2,1,0:T(8,128)(2,1)S(1)}, bf16[4,64,512]{2,1,0:T(8,128)(2,1)S(1)}, u32[]{:S(2)}, u32[]{:S(2)}) %collective-permute-start.1) | collective-permute-done | bytes 262176 | tf_op jit(solution)/shard_map/ppermute | solution.py:312
  308.5 2.9 collective-permute-done.2
  311.5 3.0 collective-permute-start.3
  317.9 2.9 collective-permute-done.11
  321.5 2.5 shard_map.238
  324.0 6.4 %all-to-all-start.16 = ((bf16[8,16,1024]{2,1,0:T(8,128)(2,1)}), bf16[8,16,1024]{2,1,0:T(8,128)(2,1)S(1)}, u32[]{:S(2)}, u32[]{:S(2)}) async-start(bf16[8,16,1024]{2,1,0:T(8,128)(2,1)} %get-tuple-element.110), calls=%async_computation.16 | async-start | bytes 524288 | tf_op jit(solution)/shard_map/all_to_all | solution.py:293
  333.9 5.1 %collective-permute-done.4 = bf16[1,64,512]{2,1,0:T(8,128)(2,1)S(1)} collective-permute-done((bf16[1,64,512]{2,1,0:T(8,128)(2,1)}, bf16[1,64,512]{2,1,0:T(8,128)(2,1)S(1)}, u32[]{:S(2)}, u32[]{:S(2)}) %collective-permute-start.4) | collective-permute-done | bytes 65568 | tf_op jit(solution)/shard_map/ppermute | solution.py:312
  347.2 5.5 %all-to-all-start.17 = ((bf16[8,24,1024]{2,1,0:T(8,128)(2,1)}), bf16[8,24,1024]{2,1,0:T(8,128)(2,1)S(1)}, u32[]{:S(2)}, u32[]{:S(2)}) async-start(bf16[8,24,1024]{2,1,0:T(8,128)(2,1)} %pad_maximum_fusion.4), calls=%async_computation.17 | async-start | bytes 786432 | tf_op jit(solution)/shard_map/all_to_all | solution.py:293
  352.7 2.8 collective-permute-start.6
  355.5 4.0 all-to-all-done.17
  362.4 10.6 %all-to-all-start.18 = ((bf16[16,8,4224]{2,1,0:T(8,128)(2,1)}), bf16[16,8,4224]{2,1,0:T(8,128)(2,1)S(1)}, u32[]{:S(2)}, u32[]{:S(2)}) async-start(bf16[16,8,4224]{2,1,0:T(8,128)(2,1)} %fusion.5), calls=%async_computation.18 | async-start | bytes 2162688 | tf_op jit(solution)/shard_map/all_to_all | solution.py:293
  373.0 2.7 collective-permute-start.14
  378.2 17.0 %collective-permute-done.14 = bf16[4,32,1024]{2,1,0:T(8,128)(2,1)S(1)} collective-permute-done((bf16[4,32,1024]{2,1,0:T(8,128)(2,1)S(1)}, bf16[4,32,1024]{2,1,0:T(8,128)(2,1)S(1)}, u32[]{:S(2)}, u32[]{:S(2)}) %collective-permute-start.14) | collective-permute-done | bytes 262176 | tf_op jit(solution)/shard_map/ppermute | solution.py:312
  398.8 7.1 %all-to-all-start.19 = ((bf16[16,8,4224]{2,1,0:T(8,128)(2,1)}), bf16[16,8,4224]{2,1,0:T(8,128)(2,1)S(1)}, u32[]{:S(2)}, u32[]{:S(2)}) async-start(bf16[16,8,4224]{2,1,0:T(8,128)(2,1)} %broadcast_in_dim.15), calls=%async_computation.19 | async-start | bytes 2162688 | tf_op jit(solution)/shard_map/all_to_all | solution.py:293
  408.3 36.5 %all-reduce.4.cloned.1.call-done = (bf16[1,1024,3,128]{3,2,1,0:T(4,128)(2,1)}, bf16[1,128,1024]{2,1,0:T(8,128)(2,1)}, bf16[1,1024,512]{2,1,0:T(8,128)(2,1)}, bf16[1,512,1024]{2,1,0:T(8,128)(2,1)}) async-done(((bf16[1,1024,3,128]{3,2,1,0:T(4,128)(2,1)}, bf16[1,128,1024]{2,1,0:T(8,128)(2,1)}, bf16[1,1024,512]{2,1,0:T(8,128)(2,1)}, bf16[1,512,1024]{2,1,0:T(8,128)(2,1)}), (bf16[1,1024,3,128]{3,2,1,0:T(4,128)(2,1)}, ...) | async-done | bytes 3145744 | tf_op jit(solution)/shard_map/psum | solution.py:548
  444.9 3.6 maximum_convert_fusion.1
  454.3 2.6 maximum_convert_fusion
  (402 shorter events, 150.5 us)
Async XLA Ops:
  9.2 71.6 %copy-start.76 = (f32[1,1024]{1,0:T(1,128)}, f32[1,1024]{1,0:T(1,128)S(1)}, u32[]{:S(2)}) copy-start(f32[1,1024]{1,0:T(1,128)S(1)} %get-tuple-element.195.gain_ref) | copy-start | bytes 12292
  12.3 28.8 %copy-start.8 = (bf16[2,128,1024]{2,1,0:T(8,128)(2,1)S(1)}, bf16[2,128,1024]{2,1,0:T(8,128)(2,1)}, u32[]{:S(2)}) copy-start(bf16[2,128,1024]{2,1,0:T(8,128)(2,1)} %w_ref.7) | copy-start | bytes 1572868
  14.6 29.1 %copy-start.52 = (bf16[128,256]{1,0:T(8,128)(2,1)}, bf16[128,256]{1,0:T(8,128)(2,1)S(1)}, u32[]{:S(2)}) copy-start(bf16[128,256]{1,0:T(8,128)(2,1)S(1)} %get-tuple-element.87.kv_ref) | copy-start | bytes 196612
  14.6 34.5 %copy-start.103 = (bf16[2,1024]{1,0:T(2,128)(2,1)S(1)}, bf16[2,1024]{1,0:T(2,128)(2,1)}, u32[]{:S(2)}) copy-start(bf16[2,1024]{1,0:T(2,128)(2,1)} %param.20) | copy-start | bytes 12292
  14.6 26.5 %all-to-all-start = ((bf16[16,128,256]{2,1,0:T(8,128)(2,1)}), bf16[16,128,256]{2,1,0:T(8,128)(2,1)S(1)}, u32[]{:S(2)}, u32[]{:S(2)}) async-start(bf16[16,128,256]{2,1,0:T(8,128)(2,1)} %copy-done.15), calls=%async_computation | async-start | bytes 2097152 | tf_op jit(solution)/shard_map/all_to_all | solution.py:293
  23.9 35.4 %copy-start.118 = (bf16[2,512]{1,0:T(2,128)(2,1)S(1)}, bf16[2,512]{1,0:T(2,128)(2,1)}, u32[]{:S(2)}) copy-start(bf16[2,512]{1,0:T(2,128)(2,1)} %param.22) | copy-start | bytes 6148
  43.7 11.1 %all-to-all-start.1 = ((bf16[8,16,1024]{2,1,0:T(8,128)(2,1)}), bf16[8,16,1024]{2,1,0:T(8,128)(2,1)S(1)}, u32[]{:S(2)}, u32[]{:S(2)}) async-start(bf16[8,16,1024]{2,1,0:T(8,128)(2,1)} %get-tuple-element.72), calls=%async_computation.1 | async-start | bytes 524288 | tf_op jit(solution)/shard_map/all_to_all | solution.py:293
  55.8 9.5 %all-to-all-start.2 = ((bf16[8,16,1024]{2,1,0:T(8,128)(2,1)}), bf16[8,16,1024]{2,1,0:T(8,128)(2,1)S(1)}, u32[]{:S(2)}, u32[]{:S(2)}) async-start(bf16[8,16,1024]{2,1,0:T(8,128)(2,1)} %get-tuple-element.73), calls=%async_computation.2 | async-start | bytes 524288 | tf_op jit(solution)/shard_map/all_to_all | solution.py:293
  71.3 9.5 %all-to-all-start.3 = ((bf16[8,16,1024]{2,1,0:T(8,128)(2,1)}), bf16[8,16,1024]{2,1,0:T(8,128)(2,1)S(1)}, u32[]{:S(2)}, u32[]{:S(2)}) async-start(bf16[8,16,1024]{2,1,0:T(8,128)(2,1)} %copy-done.41), calls=%async_computation.3 | async-start | bytes 524288 | tf_op jit(solution)/shard_map/all_to_all | solution.py:293
  94.0 39.1 %copy-start.25 = (bf16[128,128]{1,0:T(8,128)(2,1)}, bf16[128,128]{1,0:T(8,128)(2,1)S(1)}, u32[]{:S(2)}) copy-start(bf16[128,128]{1,0:T(8,128)(2,1)S(1)} %get-tuple-element.77.q_ref) | copy-start | bytes 98308
  94.0 27.2 %all-to-all-start.5 = ((bf16[16,128,256]{2,1,0:T(8,128)(2,1)}), bf16[16,128,256]{2,1,0:T(8,128)(2,1)}, u32[]{:S(2)}, u32[]{:S(2)}) async-start(bf16[16,128,256]{2,1,0:T(8,128)(2,1)} %copy-done.16), calls=%async_computation.5 | async-start | bytes 2097152 | tf_op jit(solution)/shard_map/all_to_all | solution.py:293
  103.8 41.7 %copy-start.10 = (bf16[128,1024]{1,0:T(8,128)(2,1)S(1)}, bf16[128,1024]{1,0:T(8,128)(2,1)}, u32[]{:S(2)}) copy-start(bf16[128,1024]{1,0:T(8,128)(2,1)} %g_ref.1) | copy-start | bytes 786436
  103.8 94.3 %all-gather.2.cloned.1.call-start = ((), (), s32[]{:S(2)}) async-start(), calls=%async_computation.20 | async-start | bytes 1114112 | tf_op jit(solution)/shard_map/all_gather | solution.py:432
  135.3 10.2 %all-to-all-start.7 = ((bf16[8,16,1024]{2,1,0:T(8,128)(2,1)}), bf16[8,16,1024]{2,1,0:T(8,128)(2,1)}, u32[]{:S(2)}, u32[]{:S(2)}) async-start(bf16[8,16,1024]{2,1,0:T(8,128)(2,1)} %copy-done.39), calls=%async_computation.7 | async-start | bytes 524288 | tf_op jit(solution)/shard_map/all_to_all | solution.py:293
  153.8 11.8 %all-to-all-start.8 = ((bf16[8,32,1024]{2,1,0:T(8,128)(2,1)}), bf16[8,32,1024]{2,1,0:T(8,128)(2,1)}, u32[]{:S(2)}, u32[]{:S(2)}) async-start(bf16[8,32,1024]{2,1,0:T(8,128)(2,1)} %copy-done.20), calls=%async_computation.8 | async-start | bytes 1048576 | tf_op jit(solution)/shard_map/all_to_all | solution.py:293
  160.3 22.3 %copy-start.114 = (f32[16]{0:T(128)}, f32[16]{0:T(128)S(1)}, u32[]{:S(2)}) copy-start(f32[16]{0:T(128)S(1)} %add_rsqrt_fusion) | copy-start | bytes 196
  170.7 12.5 %all-to-all-start.9 = ((bf16[8,32,1024]{2,1,0:T(8,128)(2,1)}), bf16[8,32,1024]{2,1,0:T(8,128)(2,1)}, u32[]{:S(2)}, u32[]{:S(2)}) async-start(bf16[8,32,1024]{2,1,0:T(8,128)(2,1)} %copy-done.21), calls=%async_computation.9 | async-start | bytes 1048576 | tf_op jit(solution)/shard_map/all_to_all | solution.py:293
  189.1 20.8 %all-to-all-start.10 = ((bf16[16,144,128]{2,1,0:T(8,128)(2,1)}), bf16[16,144,128]{2,1,0:T(8,128)(2,1)}, u32[]{:S(2)}, u32[]{:S(2)}) async-start(bf16[16,144,128]{2,1,0:T(8,128)(2,1)} %copy-done.19), calls=%async_computation.10 | async-start | bytes 1179648 | tf_op jit(solution)/shard_map/all_to_all | solution.py:293
  215.9 10.7 %all-to-all-start.11 = ((bf16[8,16,1024]{2,1,0:T(8,128)(2,1)}), bf16[8,16,1024]{2,1,0:T(8,128)(2,1)S(1)}, u32[]{:S(2)}, u32[]{:S(2)}) async-start(bf16[8,16,1024]{2,1,0:T(8,128)(2,1)} %copy-done.40), calls=%async_computation.11 | async-start | bytes 524288 | tf_op jit(solution)/shard_map/all_to_all | solution.py:293
  231.7 9.5 %all-to-all-start.12 = ((bf16[8,16,1024]{2,1,0:T(8,128)(2,1)}), bf16[8,16,1024]{2,1,0:T(8,128)(2,1)S(1)}, u32[]{:S(2)}, u32[]{:S(2)}) async-start(bf16[8,16,1024]{2,1,0:T(8,128)(2,1)} %copy-done.38), calls=%async_computation.12 | async-start | bytes 524288 | tf_op jit(solution)/shard_map/all_to_all | solution.py:293
  247.7 12.9 %all-to-all-start.13 = ((bf16[8,16,1024]{2,1,0:T(8,128)(2,1)}), bf16[8,16,1024]{2,1,0:T(8,128)(2,1)}, u32[]{:S(2)}, u32[]{:S(2)}) async-start(bf16[8,16,1024]{2,1,0:T(8,128)(2,1)} %copy-done.37), calls=%async_computation.13 | async-start | bytes 524288 | tf_op jit(solution)/shard_map/all_to_all | solution.py:293
  255.1 36.4 %collective-permute-start = (bf16[8,64,512]{2,1,0:T(8,128)(2,1)}, bf16[8,64,512]{2,1,0:T(8,128)(2,1)}, u32[]{:S(2)}, u32[]{:S(2)}) collective-permute-start(bf16[8,64,512]{2,1,0:T(8,128)(2,1)} %dynamic-slice_bitcast_fusion.1), channel_id=1, source_target_pairs={{0,1},{1,0},{2,3},{3,2},{4,5},{5,4},{6,7},{7,6},{8,9},{9,8},{10,11... | collective-permute-start | bytes 1572872 | tf_op jit(solution)/shard_map/ppermute | solution.py:312
  264.8 16.0 %all-to-all-start.14 = ((bf16[8,16,1024]{2,1,0:T(8,128)(2,1)}), bf16[8,16,1024]{2,1,0:T(8,128)(2,1)S(1)}, u32[]{:S(2)}, u32[]{:S(2)}) async-start(bf16[8,16,1024]{2,1,0:T(8,128)(2,1)} %copy-done.36), calls=%async_computation.14 | async-start | bytes 524288 | tf_op jit(solution)/shard_map/all_to_all | solution.py:293
  270.1 174.8 %all-reduce.4.cloned.1.call-start = ((), (), s32[]{:S(2)}) async-start(), calls=%async_computation.21 | async-start | bytes 6815744 | tf_op jit(solution)/shard_map/psum | solution.py:548
  272.0 22.3 %collective-permute-start.8 = (bf16[8,32,1024]{2,1,0:T(8,128)(2,1)}, bf16[8,32,1024]{2,1,0:T(8,128)(2,1)}, u32[]{:S(2)}, u32[]{:S(2)}) collective-permute-start(bf16[8,32,1024]{2,1,0:T(8,128)(2,1)} %dynamic-slice_bitcast_fusion), channel_id=1, source_target_pairs={{0,1},{1,0},{2,3},{3,2},{4,5},{5,4},{6,7},{7,6},{8,9},{9,8},{10,11... | collective-permute-start | bytes 1572872 | tf_op jit(solution)/shard_map/ppermute | solution.py:312
  285.4 36.1 %all-to-all-start.15 = ((bf16[16,144,128]{2,1,0:T(8,128)(2,1)}), bf16[16,144,128]{2,1,0:T(8,128)(2,1)S(1)}, u32[]{:S(2)}, u32[]{:S(2)}) async-start(bf16[16,144,128]{2,1,0:T(8,128)(2,1)} %copy-done.18), calls=%async_computation.15 | async-start | bytes 1179648 | tf_op jit(solution)/shard_map/all_to_all | solution.py:293
  292.9 12.9 %collective-permute-start.1 = (bf16[4,64,512]{2,1,0:T(8,128)(2,1)S(1)}, bf16[4,64,512]{2,1,0:T(8,128)(2,1)S(1)}, u32[]{:S(2)}, u32[]{:S(2)}) collective-permute-start(bf16[4,64,512]{2,1,0:T(8,128)(2,1)S(1)} %dynamic-slice_bitcast_fusion.3), channel_id=1, source_target_pairs={{0,4},{1,5},{2,6},{3,7},{4,0},{5,1},{6,2},{7,3},{8,12},{9,13},{10,... | collective-permute-start | bytes 786440 | tf_op jit(solution)/shard_map/ppermute | solution.py:312
  295.6 25.9 %copy-start.13 = (bf16[2048,128]{1,0:T(8,128)(2,1)S(1)}, bf16[2048,128]{1,0:T(8,128)(2,1)}, u32[]{:S(2)}) copy-start(bf16[2048,128]{1,0:T(8,128)(2,1)} %get-tuple-element.160.q_ref) | copy-start | bytes 1572868
  295.6 25.9 %copy-start.53 = (bf16[128,256]{1,0:T(8,128)(2,1)S(1)}, bf16[128,256]{1,0:T(8,128)(2,1)}, u32[]{:S(2)}) copy-start(bf16[128,256]{1,0:T(8,128)(2,1)} %copy-done.52) | copy-start | bytes 196612
  295.6 11.0 %collective-permute-start.9 = (bf16[4,32,1024]{2,1,0:T(8,128)(2,1)S(1)}, bf16[4,32,1024]{2,1,0:T(8,128)(2,1)S(1)}, u32[]{:S(2)}, u32[]{:S(2)}) collective-permute-start(bf16[4,32,1024]{2,1,0:T(8,128)(2,1)S(1)} %dynamic-slice_bitcast_fusion.2), channel_id=1, source_target_pairs={{0,12},{1,13},{2,14},{3,15},{4,8},{5,9},{6,10},{7,11},{8,4},{9,5},... | collective-permute-start | bytes 786440 | tf_op jit(solution)/shard_map/ppermute | solution.py:312
  305.9 5.5 %collective-permute-start.2 = (bf16[2,64,512]{2,1,0:T(8,128)(2,1)S(1)}, bf16[2,64,512]{2,1,0:T(8,128)(2,1)S(1)}, u32[]{:S(2)}, u32[]{:S(2)}) collective-permute-start(bf16[2,64,512]{2,1,0:T(8,128)(2,1)S(1)} %dynamic-slice_bitcast_fusion.5), channel_id=1, source_target_pairs={{0,12},{1,13},{2,14},{3,15},{4,8},{5,9},{6,10},{7,11},{8,4},{9,5},... | collective-permute-start | bytes 393224 | tf_op jit(solution)/shard_map/ppermute | solution.py:312
  306.7 7.8 %collective-permute-start.10 = (bf16[2,32,1024]{2,1,0:T(8,128)(2,1)S(1)}, bf16[2,32,1024]{2,1,0:T(8,128)(2,1)S(1)}, u32[]{:S(2)}, u32[]{:S(2)}) collective-permute-start(bf16[2,32,1024]{2,1,0:T(8,128)(2,1)S(1)} %dynamic-slice_bitcast_fusion.4), channel_id=1, source_target_pairs={{0,4},{1,5},{2,6},{3,7},{4,0},{5,1},{6,2},{7,3},{8,12},{9,13},{10,... | collective-permute-start | bytes 393224 | tf_op jit(solution)/shard_map/ppermute | solution.py:312
  311.5 5.8 %collective-permute-start.3 = (bf16[1,64,512]{2,1,0:T(8,128)(2,1)S(1)}, bf16[1,64,512]{2,1,0:T(8,128)(2,1)S(1)}, u32[]{:S(2)}, u32[]{:S(2)}) collective-permute-start(bf16[1,64,512]{2,1,0:T(8,128)(2,1)S(1)} %constant_dynamic-slice_fusion.1), channel_id=1, source_target_pairs={{0,2},{1,3},{2,0},{3,1},{4,6},{5,7},{6,4},{7,5},{8,10},{9,11},{10,... | collective-permute-start | bytes 196616 | tf_op jit(solution)/shard_map/ppermute | solution.py:312
  314.5 6.3 %collective-permute-start.11 = (bf16[1,32,1024]{2,1,0:T(8,128)(2,1)S(1)}, bf16[1,32,1024]{2,1,0:T(8,128)(2,1)S(1)}, u32[]{:S(2)}, u32[]{:S(2)}) collective-permute-start(bf16[1,32,1024]{2,1,0:T(8,128)(2,1)S(1)} %constant_dynamic-slice_fusion), channel_id=1, source_target_pairs={{0,2},{1,3},{2,0},{3,1},{4,6},{5,7},{6,4},{7,5},{8,10},{9,11},{10,... | collective-permute-start | bytes 196616 | tf_op jit(solution)/shard_map/ppermute | solution.py:312
  324.0 22.3 %copy-start.105 = (bf16[2,1024]{1,0:T(2,128)(2,1)S(1)}, bf16[2,1024]{1,0:T(2,128)(2,1)}, u32[]{:S(2)}) copy-start(bf16[2,1024]{1,0:T(2,128)(2,1)} %convert.61) | copy-start | bytes 12292
  324.0 22.3 %copy-start.106 = (bf16[2,1024]{1,0:T(2,128)(2,1)S(1)}, bf16[2,1024]{1,0:T(2,128)(2,1)}, u32[]{:S(2)}) copy-start(bf16[2,1024]{1,0:T(2,128)(2,1)} %convert.59) | copy-start | bytes 12292
  324.0 21.4 %all-to-all-start.16 = ((bf16[8,16,1024]{2,1,0:T(8,128)(2,1)}), bf16[8,16,1024]{2,1,0:T(8,128)(2,1)S(1)}, u32[]{:S(2)}, u32[]{:S(2)}) async-start(bf16[8,16,1024]{2,1,0:T(8,128)(2,1)} %get-tuple-element.110), calls=%async_computation.16 | async-start | bytes 524288 | tf_op jit(solution)/shard_map/all_to_all | solution.py:293
  330.8 8.2 %collective-permute-start.4 = (bf16[1,64,512]{2,1,0:T(8,128)(2,1)}, bf16[1,64,512]{2,1,0:T(8,128)(2,1)S(1)}, u32[]{:S(2)}, u32[]{:S(2)}) collective-permute-start(bf16[1,64,512]{2,1,0:T(8,128)(2,1)} %add_convert_fusion.1), channel_id=1, source_target_pairs={{0,2},{1,3},{2,0},{3,1},{4,6},{5,7},{6,4},{7,5},{8,10},{9,11},{10,... | collective-permute-start | bytes 196616 | tf_op jit(solution)/shard_map/ppermute | solution.py:312
  332.8 10.0 %collective-permute-start.12 = (bf16[1,32,1024]{2,1,0:T(8,128)(2,1)}, bf16[1,32,1024]{2,1,0:T(8,128)(2,1)S(1)}, u32[]{:S(2)}, u32[]{:S(2)}) collective-permute-start(bf16[1,32,1024]{2,1,0:T(8,128)(2,1)} %add_convert_fusion), channel_id=1, source_target_pairs={{0,2},{1,3},{2,0},{3,1},{4,6},{5,7},{6,4},{7,5},{8,10},{9,11},{10,... | collective-permute-start | bytes 196616 | tf_op jit(solution)/shard_map/ppermute | solution.py:312
  339.9 5.5 %collective-permute-start.5 = (bf16[2,64,512]{2,1,0:T(8,128)(2,1)S(1)}, bf16[2,64,512]{2,1,0:T(8,128)(2,1)S(1)}, u32[]{:S(2)}, u32[]{:S(2)}) collective-permute-start(bf16[2,64,512]{2,1,0:T(8,128)(2,1)S(1)} %pad_maximum_fusion.7), channel_id=1, source_target_pairs={{0,12},{1,13},{2,14},{3,15},{4,8},{5,9},{6,10},{7,11},{8,4},{9,5},... | collective-permute-start | bytes 393224 | tf_op jit(solution)/shard_map/ppermute | solution.py:312
  342.9 12.6 %collective-permute-start.13 = (bf16[2,32,1024]{2,1,0:T(8,128)(2,1)S(1)}, bf16[2,32,1024]{2,1,0:T(8,128)(2,1)S(1)}, u32[]{:S(2)}, u32[]{:S(2)}) collective-permute-start(bf16[2,32,1024]{2,1,0:T(8,128)(2,1)S(1)} %pad_maximum_fusion.8), channel_id=1, source_target_pairs={{0,4},{1,5},{2,6},{3,7},{4,0},{5,1},{6,2},{7,3},{8,12},{9,13},{10,... | collective-permute-start | bytes 393224 | tf_op jit(solution)/shard_map/ppermute | solution.py:312
  347.2 12.4 %all-to-all-start.17 = ((bf16[8,24,1024]{2,1,0:T(8,128)(2,1)}), bf16[8,24,1024]{2,1,0:T(8,128)(2,1)S(1)}, u32[]{:S(2)}, u32[]{:S(2)}) async-start(bf16[8,24,1024]{2,1,0:T(8,128)(2,1)} %pad_maximum_fusion.4), calls=%async_computation.17 | async-start | bytes 786432 | tf_op jit(solution)/shard_map/all_to_all | solution.py:293
  352.7 23.0 %collective-permute-start.6 = (bf16[4,64,512]{2,1,0:T(8,128)(2,1)S(1)}, bf16[4,64,512]{2,1,0:T(8,128)(2,1)}, u32[]{:S(2)}, u32[]{:S(2)}) collective-permute-start(bf16[4,64,512]{2,1,0:T(8,128)(2,1)S(1)} %pad_maximum_fusion.5), channel_id=1, source_target_pairs={{0,4},{1,5},{2,6},{3,7},{4,0},{5,1},{6,2},{7,3},{8,12},{9,13},{10,... | collective-permute-start | bytes 786440 | tf_op jit(solution)/shard_map/ppermute | solution.py:312
  362.4 35.2 %all-to-all-start.18 = ((bf16[16,8,4224]{2,1,0:T(8,128)(2,1)}), bf16[16,8,4224]{2,1,0:T(8,128)(2,1)S(1)}, u32[]{:S(2)}, u32[]{:S(2)}) async-start(bf16[16,8,4224]{2,1,0:T(8,128)(2,1)} %fusion.5), calls=%async_computation.18 | async-start | bytes 2162688 | tf_op jit(solution)/shard_map/all_to_all | solution.py:293
  373.0 22.2 %collective-permute-start.14 = (bf16[4,32,1024]{2,1,0:T(8,128)(2,1)S(1)}, bf16[4,32,1024]{2,1,0:T(8,128)(2,1)S(1)}, u32[]{:S(2)}, u32[]{:S(2)}) collective-permute-start(bf16[4,32,1024]{2,1,0:T(8,128)(2,1)S(1)} %pad_maximum_fusion.6), channel_id=1, source_target_pairs={{0,12},{1,13},{2,14},{3,15},{4,8},{5,9},{6,10},{7,11},{8,4},{9,5},... | collective-permute-start | bytes 786440 | tf_op jit(solution)/shard_map/ppermute | solution.py:312
  377.5 28.4 %collective-permute-start.7 = (bf16[8,64,512]{2,1,0:T(8,128)(2,1)}, bf16[8,64,512]{2,1,0:T(8,128)(2,1)}, u32[]{:S(2)}, u32[]{:S(2)}) collective-permute-start(bf16[8,64,512]{2,1,0:T(8,128)(2,1)} %pad_maximum_fusion.2), channel_id=1, source_target_pairs={{0,1},{1,0},{2,3},{3,2},{4,5},{5,4},{6,7},{7,6},{8,9},{9,8},{10,11... | collective-permute-start | bytes 1572872 | tf_op jit(solution)/shard_map/ppermute | solution.py:312
  396.1 11.0 %collective-permute-start.15 = (bf16[8,32,1024]{2,1,0:T(8,128)(2,1)}, bf16[8,32,1024]{2,1,0:T(8,128)(2,1)}, u32[]{:S(2)}, u32[]{:S(2)}) collective-permute-start(bf16[8,32,1024]{2,1,0:T(8,128)(2,1)} %pad_maximum_fusion.3), channel_id=1, source_target_pairs={{0,1},{1,0},{2,3},{3,2},{4,5},{5,4},{6,7},{7,6},{8,9},{9,8},{10,11... | collective-permute-start | bytes 1572872 | tf_op jit(solution)/shard_map/ppermute | solution.py:312
  398.8 52.0 %all-to-all-start.19 = ((bf16[16,8,4224]{2,1,0:T(8,128)(2,1)}), bf16[16,8,4224]{2,1,0:T(8,128)(2,1)S(1)}, u32[]{:S(2)}, u32[]{:S(2)}) async-start(bf16[16,8,4224]{2,1,0:T(8,128)(2,1)} %broadcast_in_dim.15), calls=%async_computation.19 | async-start | bytes 2162688 | tf_op jit(solution)/shard_map/all_to_all | solution.py:293
  (107 other events, 642.3 us)
Sparse Core Ops, SparseCore 0:
  107.1 45.0 all-gather.1
  276.4 168.3 all-reduce.3
where the time goes:
time: 471 us; the launch traced here: 467 us
  waiting for transfers between devices  152 us (32%)
  starting transfers between devices  131 us (28%)
  local copies, waits for them, and re-layouts  69.2 us (15%)
  other arithmetic  43 us (9%)
  Pallas kernels  25.2 us (5%)
  blocking collectives  17.3 us (4%)
  between operations  15.3 us (3%)
  matrix products  13.8 us (3%)
    all_to_all x18, starting transfers between devices, swap_all(): return lax.all_to_all(value, axis, 0, 0)  102 us
    all_to_all x18, waiting for transfers between devices, swap_all(): return lax.all_to_all(value, axis, 0, 0)  76 us
    unnamed x251, local copies, waits for them, and re-layouts  56 us
    ppermute x16, waiting for transfers between devices, swap(): return lax.ppermute(value, 'dp', [(i, i ^ flip) for i in range(count)])  39.7 us
    psum x1, waiting for transfers between devices, body(): done[layer] = lax.psum(big, 'dp')  36.5 us
    ppermute x16, starting transfers between devices, swap(): return lax.ppermute(value, 'dp', [(i, i ^ flip) for i in range(count)])  28.1 us
    pallas_call x20, Pallas kernels, call(): pl.pallas_call(kernel, grid=(1,), in_specs=[spec(index, arg) for index, a...  25.2 us
    all_to_all x2, blocking collectives, swap_all(): return lax.all_to_all(value, axis, 0, 0)  17.3 us
  transfers between devices with their start and end apart: 36, of which 20 were waited for; matrix products, arithmetic and copies ran while one was open for 14% of the time, Pallas kernels for 3%

commit v1 on v0

--- a/solution.py
+++ b/solution.py
@@ -44,12 +44,19 @@
     return 0.5 * (1.0 + bend) + 0.5 * value * (1.0 - bend * bend) * inner
 
 
-def call(kernel, outs, layered, *args):
+def call(kernel, outs, layered, *args, room=12, blocks={}):
     layer, wide = layered
+    near = NEAR.get(kernel, ())
+    args = [
+        arg if index in near or arg.shape == (1,) else pltpu.with_memory_space_constraint(arg, pltpu.HBM)
+        for index, arg in enumerate(args)
+    ]
 
     def spec(index, arg):
         if arg.dtype == jnp.int32 and arg.shape == (1,):
             return pl.BlockSpec(memory_space=pltpu.SMEM)
+        if index in blocks:
+            return pl.BlockSpec(*blocks[index])
         if index in wide:
             rest = arg.shape[1:]
             return pl.BlockSpec((None,) + rest, lambda i: (layer,) + (0,) * len(rest))
@@ -60,8 +67,9 @@
         grid=(1,),
         in_specs=[spec(index, arg) for index, arg in enumerate(args)],
         out_specs=[pl.BlockSpec(out.shape, lambda i, n=len(out.shape): (0,) * n) for out in outs],
-        out_shape=outs,
-        compiler_params=pltpu.CompilerParams(vmem_limit_bytes=40 * 1024 * 1024),
+        out_shape=[pltpu.HBM(out.shape, out.dtype) for out in outs],
+        cost_estimate=pl.CostEstimate(flops=1000, bytes_accessed=1000, transcendentals=0),
+        compiler_params=pltpu.CompilerParams(vmem_limit_bytes=room * 1024 * 1024),
     )(*args)
 
 
@@ -219,7 +227,7 @@
 
 def output_back_kernel(gy_ref, w_ref, o_ref, log_ref, go_ref, delta_ref, sent_ref):
     rows, local = o_ref.shape
-    g_o = dot_t(gy_ref[...], w_ref[...]).astype(BF16)
+    g_o = dot_t(gy_ref[...].reshape(rows, -1), w_ref[...]).astype(BF16)
     go_ref[...] = g_o
     masks = head_masks(rows, local)
     product = g_o.astype(F32) * o_ref[...]
@@ -289,36 +297,74 @@
     part_ref[...] = part.astype(BF16).reshape(part_ref.shape)
 
 
+def end_grads_kernel(h_ref, gm_ref, b_ref, gf_ref, proj_ref, fc_ref, gm_sum, gf_sum):
+    g_m = gm_ref[...].reshape(-1, gm_ref.shape[-1])
+    g_f = gf_ref[...]
+    proj_ref[...] = cross(h_ref[...], g_m).astype(BF16)
+    fc_ref[...] = cross(b_ref[...], g_f).astype(BF16)
+    gm_sum[...] = jnp.sum(g_m.astype(F32), 0, keepdims=True)
+    gf_sum[...] = jnp.sum(g_f.astype(F32), 0, keepdims=True)
+
+
+def attend_grads_kernel(o_ref, gy_ref, a_ref, gq_ref, gkv_ref, out_ref, qkv_ref, gy_sum, gq_sum, gv_sum):
+    local = gq_ref.shape[1]
+    g_y = gy_ref[...].reshape(-1, gy_ref.shape[-1])
+    a_low = a_ref[...]
+    g_q, g_v = gq_ref[...], gkv_ref[:, local:]
+    out_ref[...] = cross(o_ref[...], g_y).astype(BF16)
+    qkv_ref[0] = cross(a_low, g_q).astype(BF16)
+    qkv_ref[1] = cross(a_low, gkv_ref[:, :local]).astype(BF16)
+    qkv_ref[2] = cross(a_low, g_v).astype(BF16)
+    gy_sum[...] = jnp.sum(g_y.astype(F32), 0, keepdims=True)
+    gq_sum[...] = jnp.sum(g_q.astype(F32), 0, keepdims=True)
+    gv_sum[...] = jnp.sum(g_v.astype(F32), 0, keepdims=True)
+
+
+NEAR = {
+    project_kernel: (0,),
+    attend_kernel: (4,),
+    row_kernel: (0,),
+    forward_kernel: (0,),
+    turn_kernel: (0,),
+    turn_back_kernel: (0,),
+    back_kernel: (0,),
+    backward_kernel: (0,),
+    output_back_kernel: (0,),
+    query_back_kernel: (4,),
+    key_back_kernel: (5,),
+    end_grads_kernel: (1, 2),
+    attend_grads_kernel: (1, 2),
+}
+
+
 def swap_all(value, axis):
     return lax.all_to_all(value, axis, 0, 0)
 
 
-def column_sum(value):
-    return jnp.sum(value.astype(F32), 0)
-
-
 def cross(left, right):
     return lax.dot_general(left, right, (((0,), (0,)), ((), ())), preferred_element_type=F32)
 
 
-def pair_sums(parts, turn, after):
+def pair_sums(parts, turn, events):
     place = lax.axis_index("dp")
     count = lax.axis_size("dp")
     x_low, x_high = (place // 4) % 2, place // 8
     along_x = ((x_low ^ x_high, 4), (x_high, 12)) if turn else ((x_high, 12), (x_low ^ x_high, 4))
     steps = ((place % 2, 1),) + along_x + (((place // 2) % 2, 2),)
-
-    def swap(value, flip):
-        return lax.ppermute(value, "dp", [(i, i ^ flip) for i in range(count)])
-
-    for bit, flip in steps:
+    y_here, keys_done, rows_done, tail_done = events
+    waits = (y_here, keys_done, rows_done, tail_done, None, None, None, None)
+
+    def swap(value, flip, wait):
+        got = lax.ppermute(value, "dp", [(i, i ^ flip) for i in range(count)])
+        return got if wait is None else lax.optimization_barrier((got, wait))[0]
+
+    for (bit, flip), wait in zip(steps, waits):
         halves = parts.reshape((2, -1) + parts.shape[1:])
         mine = lax.dynamic_index_in_dim(halves, bit, 0, keepdims=False)
         other = lax.dynamic_index_in_dim(halves, 1 - bit, 0, keepdims=False)
-        parts = (mine.astype(F32) + swap(other, flip).astype(F32)).astype(BF16)
-    parts = lax.optimization_barrier((parts, after))[0]
-    for bit, flip in reversed(steps):
-        got = swap(parts, flip)
+        parts = (mine.astype(F32) + swap(other, flip, wait).astype(F32)).astype(BF16)
+    for (bit, flip), wait in zip(reversed(steps), waits[4:]):
+        got = swap(parts, flip, wait)
         parts = jnp.concatenate((jnp.where(bit, got, parts), jnp.where(bit, parts, got)), 0)
     return parts
 
@@ -393,6 +439,7 @@
             q_low,
             kv_all,
             w_out,
+            room=24,
         )
         middle, b_normed, b_factor, b_sent = call(
             row_kernel,
@@ -436,6 +483,25 @@
     smalls, sums = [], []
     two_rows = shape((2, width), F32)
     out = None
+    events = []
+
+    def end_grads(layer, h_low, g_m, b_low, g_f):
+        return call(
+            end_grads_kernel,
+            [
+                shape((hidden, width), BF16),
+                shape((width, hidden), BF16),
+                shape((1, width), F32),
+                shape((1, hidden), F32),
+            ],
+            (layer, ()),
+            h_low,
+            g_m,
+            b_low,
+            g_f,
+            room=16,
+        )
+
     for layer in reversed(range(layers)):
         a_normed, a_factor, a_low, q_low, kv_own, kv_all, o_full, o_low, logs, b_normed, b_factor, b_low = (
             saved[layer][:12]
@@ -465,7 +531,7 @@
                 grad,
             )
             got = swap_all(sent, "tensor")
-            g_y = got[:, :share].reshape(rows, width)
+            g_y = got
             out = got[:, share:].reshape(rows, width).astype(F32)
         else:
             pre, h_low = saved[layer][12:]
@@ -478,6 +544,7 @@
                 w_fc,
                 w_proj,
             )
+            g_w_proj, g_w_fc, gm_sum, gf_sum = end_grads(layer, h_low, g_m, b_low, g_f)
             grad, sums_b, sent = call(
                 back_kernel,
                 [row_block, two_rows, exchange],
@@ -488,7 +555,8 @@
                 gains[layer, 1],
                 grad,
             )
-            g_y = swap_all(sent, "tensor").reshape(rows, width)
+            g_y = swap_all(sent, "tensor")
+            events.append(g_y)
         g_o, delta, sent = call(
             output_back_kernel,
             [shape((rows, local), BF16), shape((rows, local), F32), shape((ranks, rows + 16, local), BF16)],
@@ -497,6 +565,7 @@
             w_out,
             o_full,
             logs,
+            blocks={0: ((slots, share, width), lambda i: (0, 0, 0))},
         )
         go_all = swap_all(sent, "dp")
         (g_q,) = call(
@@ -509,6 +578,7 @@
             g_o,
             logs,
             delta,
+            room=24,
         )
         g_kv, parts = call(
             key_back_kernel,
@@ -516,10 +586,12 @@
             (layer, (7,)),
             *spots,
             kv_own,
-            q_every[:, layer * local : (layer + 1) * local],
+            q_every,
             go_all,
             g_q,
             w_three,
+            room=24,
+            blocks={4: ((total, local), lambda i: (0, layer))},
         )
         grad, sums_a, sent = call(
             back_kernel,
@@ -532,43 +604,56 @@
             grad,
         )
         sums = [sums_a, sums_b] + sums
-        smalls = [
-            column_sum(g_y),
-            column_sum(g_m),
-            column_sum(g_q),
-            column_sum(g_kv[:, local:]),
-            column_sum(g_f),
-        ] + smalls
-        g_w_qkv = cross(a_low, jnp.concatenate((g_q, g_kv), 1))
-        big = tuple(
-            part.astype(BF16) for part in (cross(h_low, g_m), cross(b_low, g_f), cross(o_low, g_y), g_w_qkv)
-        )
         if layer:
-            g_m = swap_all(sent, "tensor").reshape(rows, width)
+            g_w_proj, g_w_fc, gm_sum, gf_sum = end_grads(layer, h_low, g_m, b_low, g_f)
+        g_w_out, g_w_qkv, gy_sum, gq_sum, gv_sum = call(
+            attend_grads_kernel,
+            [
+                shape((local, width), BF16),
+                shape((3, width, local), BF16),
+                shape((1, width), F32),
+                shape((1, local), F32),
+                shape((1, local), F32),
+            ],
+            (layer, ()),
+            o_low,
+            g_y,
+            a_low,
+            g_q,
+            g_kv,
+            room=16,
+            blocks={1: ((slots, share, width), lambda i: (0, 0, 0))},
+        )
+        smalls = [gy_sum, gm_sum, gq_sum, gv_sum, gf_sum] + smalls
+        if layer:
+            big = (g_w_proj, g_w_fc, g_w_out, g_w_qkv)
+            g_m, big = lax.optimization_barrier((swap_all(sent, "tensor").reshape(rows, width), big))
             done[layer] = lax.psum(big, "dp")
-    early = tuple(
-        pair_sums(part.reshape(ranks, -1, part.shape[1]), turn, g_kv).reshape(part.shape)
-        for turn, part in enumerate(big[:2])
-    )
     tail = jnp.concatenate([sent, jnp.broadcast_to(jnp.concatenate(sums, 0).astype(BF16), (slots, 8, width))], 1)
-    got = swap_all(tail, "tensor")
+    tail_got = got = swap_all(tail, "tensor")
     grad_input = got[:, :share].reshape(rows, width).astype(F32)
     norm_sums = jnp.sum(got[:, share:].astype(F32), 0)
-    small = jnp.concatenate([norm_sums.reshape(-1)] + smalls)
+    small = jnp.concatenate([norm_sums.reshape(-1)] + [part.reshape(-1) for part in smalls])
     each = small.size // (8 * ranks)
     wide = 4 * width
     packed = jnp.concatenate(
         (
-            big[2].reshape(ranks, 8, width),
-            big[3].reshape(ranks, 8, 8, 3 * local).transpose(0, 2, 1, 3).reshape(ranks, 8, 3 * width),
+            g_w_out.reshape(ranks, 8, width),
+            g_w_qkv.reshape(3, ranks, 8, 8, local).transpose(1, 3, 0, 2, 4).reshape(ranks, 8, 3 * width),
             jnp.pad(small.astype(BF16).reshape(ranks, 8, each), ((0, 0), (0, 0), (0, 128 - each))),
         ),
         2,
     )
-    mine = jnp.sum(swap_all(packed, "dp").astype(F32), 0).astype(BF16)
+    arrived = swap_all(packed, "dp")
+    events += [g_kv, grad, tail_got]
+    early = tuple(
+        pair_sums(part.reshape(ranks, -1, part.shape[1]), turn, events).reshape(part.shape)
+        for turn, part in enumerate((g_w_proj, g_w_fc))
+    )
+    mine = jnp.sum(arrived.astype(F32), 0).astype(BF16)
     got = swap_all(jnp.broadcast_to(mine, (ranks,) + mine.shape), "dp")
-    late_out = got[:, :, :width].reshape(big[2].shape)
-    late_qkv = got[:, :, width:wide].reshape(ranks, 8, 8, 3 * local).transpose(0, 2, 1, 3).reshape(big[3].shape)
+    late_out = got[:, :, :width].reshape(g_w_out.shape)
+    late_qkv = got[:, :, width:wide].reshape(ranks, 8, 3, 8, local).transpose(2, 0, 3, 1, 4).reshape(g_w_qkv.shape)
     done[0] = early + (late_out, late_qkv)
     small = got[:, :, wide : wide + each].reshape(-1).astype(F32)
     norm_grads = small[: 8 * width].reshape(layers, 2, 2, width)
@@ -583,7 +668,7 @@
         grad_input,
         norm_grads[:, :, 0],
         norm_grads[:, :, 1],
-        both(3).reshape(layers, width, 3, local),
+        both(3).transpose(0, 2, 1, 3),
         per_layer[:, cut : cut + 2 * local].reshape(layers, 2, local),
         both(2),
         per_layer[:, :width],

time: 471 us -> 440 us (0.934)
  local copies, waits for them, and re-layouts: 69.2 us -> 17.8 us
  Pallas kernels: 25.2 us -> 63.4 us
  blocking collectives: 17.3 us -> 45.6 us
  starting transfers between devices: 131 us -> 103 us
  matrix products: 13.8 us -> 0 us
  other arithmetic: 43 us -> 32.8 us
  waiting for transfers between devices: 152 us -> 157 us
    unnamed x251 -> x60, local copies, waits for them, and re-layouts: 56 us -> 4.55 us
    pallas_call x20 -> x24, Pallas kernels: 25.2 us -> 63.4 us  [call(): pl.pallas_call(kernel, grid=(1,), in_specs=[spec(index, arg) for index, a...]
    all_to_all x2 -> x3, blocking collectives: 17.3 us -> 45.6 us  [swap_all(): return lax.all_to_all(value, axis, 0, 0)]
    all_to_all x18 -> x17, starting transfers between devices: 102 us -> 80.9 us  [swap_all(): return lax.all_to_all(value, axis, 0, 0)]
    psum x1, waiting for transfers between devices: 36.5 us -> 56.3 us  [body(): done[layer] = lax.psum(big, 'dp')]
    dot_general x8 -> x0, matrix products: 13.8 us -> none  [cross(): lax.dot_general(left, right, (((0,), (0,)), ((), ())), preferred_element_...]
    ppermute x16, waiting for transfers between devices: 39.7 us -> 26.8 us  [swap(): got = lax.ppermute(value, 'dp', [(i, i ^ flip) for i in range(count)])]
    reduce_sum x11 -> x1, other arithmetic: 10.8 us -> 0.15 us  [body(): mine = jnp.sum(arrived.astype(F32), 0).astype(BF16)]
  transfers between devices with their start and end apart: 36 -> 35, of which waited for: 20 -> 19; matrix products, arithmetic and copies ran while one was open for 14% -> 9% of each run, Pallas kernels for 3% -> 8%
where the time goes in v1:
time: 440 us; the launch traced here: 434 us
  waiting for transfers between devices  157 us (36%)
  starting transfers between devices  103 us (23%)
  Pallas kernels  63.4 us (14%)
  blocking collectives  45.6 us (10%)
  other arithmetic  32.8 us (7%)
  local copies, waits for them, and re-layouts  17.8 us (4%)
  between operations  14.9 us (3%)
    all_to_all x17, starting transfers between devices, swap_all(): return lax.all_to_all(value, axis, 0, 0)  80.9 us
    all_to_all x17, waiting for transfers between devices, swap_all(): return lax.all_to_all(value, axis, 0, 0)  73.6 us
    pallas_call x24, Pallas kernels, call(): pl.pallas_call(kernel, grid=(1,), in_specs=[spec(index, arg) for index, a...  63.4 us
    psum x1, waiting for transfers between devices, body(): done[layer] = lax.psum(big, 'dp')  56.3 us
    all_to_all x3, blocking collectives, swap_all(): return lax.all_to_all(value, axis, 0, 0)  45.6 us
    ppermute x16, waiting for transfers between devices, swap(): got = lax.ppermute(value, 'dp', [(i, i ^ flip) for i in range(count)])  26.8 us
    ppermute x16, starting transfers between devices, swap(): got = lax.ppermute(value, 'dp', [(i, i ^ flip) for i in range(count)])  22.1 us
  transfers between devices with their start and end apart: 35, of which 19 were waited for; matrix products, arithmetic and copies ran while one was open for 9% of the time, Pallas kernels for 8%

profile of v1, /device:TPU:1, one launch (start us, length us, event | category | flops | bytes accessed | tf_op | source)
XLA Modules:
  0.0 434.4 jit_solution(14930183812966013934)
XLA Ops:
  9.2 2.9 shard_map.220
  12.1 9.3 %all-to-all-start = ((bf16[16,128,256]{2,1,0:T(8,128)(2,1)}), bf16[16,128,256]{2,1,0:T(8,128)(2,1)S(1)}, u32[]{:S(2)}, u32[]{:S(2)}) async-start(bf16[16,128,256]{2,1,0:T(8,128)(2,1)} %get-tuple-element.101), calls=%async_computation | async-start | bytes 2097152 | tf_op jit(solution)/shard_map/all_to_all | solution.py:341
  22.9 15.7 %all-to-all-done.kv_ref = bf16[16,128,256]{2,1,0:T(8,128)(2,1)S(1)} async-done(((bf16[16,128,256]{2,1,0:T(8,128)(2,1)}), bf16[16,128,256]{2,1,0:T(8,128)(2,1)S(1)}, u32[]{:S(2)}, u32[]{:S(2)}) %all-to-all-start) | async-done | bytes 1048608 | tf_op jit(solution)/shard_map/all_to_all | solution.py:341
  38.6 3.6 shard_map.221
  42.2 4.7 %all-to-all-start.1 = ((bf16[8,16,1024]{2,1,0:T(8,128)(2,1)}), bf16[8,16,1024]{2,1,0:T(8,128)(2,1)S(1)}, u32[]{:S(2)}, u32[]{:S(2)}) async-start(bf16[8,16,1024]{2,1,0:T(8,128)(2,1)} %get-tuple-element.102), calls=%async_computation.1 | async-start | bytes 524288 | tf_op jit(solution)/shard_map/all_to_all | solution.py:341
  48.8 4.5 %all-to-all-done.1.parts_ref = bf16[8,16,1024]{2,1,0:T(8,128)(2,1)S(1)} async-done(((bf16[8,16,1024]{2,1,0:T(8,128)(2,1)}), bf16[8,16,1024]{2,1,0:T(8,128)(2,1)S(1)}, u32[]{:S(2)}, u32[]{:S(2)}) %all-to-all-start.1) | async-done | bytes 262176 | tf_op jit(solution)/shard_map/all_to_all | solution.py:341
  55.1 3.4 all-to-all-start.2
  59.2 5.5 %all-to-all-done.2 = bf16[8,16,1024]{2,1,0:T(8,128)(2,1)S(1)} async-done(((bf16[8,16,1024]{2,1,0:T(8,128)(2,1)}), bf16[8,16,1024]{2,1,0:T(8,128)(2,1)S(1)}, u32[]{:S(2)}, u32[]{:S(2)}) %all-to-all-start.2) | async-done | bytes 262176 | tf_op jit(solution)/shard_map/all_to_all | solution.py:341
  64.6 2.9 shard_map.223
  67.5 3.4 all-to-all-start.3
  71.5 5.5 %all-to-all-done.3.parts_ref = bf16[8,16,1024]{2,1,0:T(8,128)(2,1)S(1)} async-done(((bf16[8,16,1024]{2,1,0:T(8,128)(2,1)}), bf16[8,16,1024]{2,1,0:T(8,128)(2,1)S(1)}, u32[]{:S(2)}, u32[]{:S(2)}) %all-to-all-start.3) | async-done | bytes 262176 | tf_op jit(solution)/shard_map/all_to_all | solution.py:341
  78.8 9.5 %all_to_all.100 = bf16[8,16,1024]{2,1,0:T(8,128)(2,1)S(1)} all-to-all(bf16[8,16,1024]{2,1,0:T(8,128)(2,1)} %get-tuple-element.106), channel_id=1, replica_groups=mesh['tensor'=8,'dp'=16] {'tensor'}, dimensions={0} | all-to-all | bytes 524288 | tf_op jit(solution)/shard_map/all_to_all | solution.py:341
  90.9 26.6 %all_to_all.101.kv_ref = bf16[16,128,256]{2,1,0:T(8,128)(2,1)S(1)} all-to-all(bf16[16,128,256]{2,1,0:T(8,128)(2,1)} %get-tuple-element.108), channel_id=1, replica_groups=mesh['tensor'=8,'dp'=16] {'dp'}, dimensions={0} | all-to-all | bytes 2097152 | tf_op jit(solution)/shard_map/all_to_all | solution.py:341
  117.5 3.6 shard_map.226
  121.1 3.4 all-to-all-start.6
  125.3 5.7 %all-to-all-done.6.parts_ref = bf16[8,16,1024]{2,1,0:T(8,128)(2,1)S(1)} async-done(((bf16[8,16,1024]{2,1,0:T(8,128)(2,1)}), bf16[8,16,1024]{2,1,0:T(8,128)(2,1)S(1)}, u32[]{:S(2)}, u32[]{:S(2)}) %all-to-all-start.6) | async-done | bytes 262176 | tf_op jit(solution)/shard_map/all_to_all | solution.py:341
  132.8 9.6 %all_to_all.102 = bf16[8,16,1024]{2,1,0:T(8,128)(2,1)S(1)} all-to-all(bf16[8,16,1024]{2,1,0:T(8,128)(2,1)} %get-tuple-element.111), channel_id=1, replica_groups=mesh['tensor'=8,'dp'=16] {'tensor'}, dimensions={0} | all-to-all | bytes 524288 | tf_op jit(solution)/shard_map/all_to_all | solution.py:341
  142.3 3.7 shard_map.228
  146.1 3.5 all-to-all-start.8
  151.0 6.2 %all-to-all-done.8.parts_ref = bf16[8,32,1024]{2,1,0:T(8,128)(2,1)S(1)} async-done(((bf16[8,32,1024]{2,1,0:T(8,128)(2,1)}), bf16[8,32,1024]{2,1,0:T(8,128)(2,1)S(1)}, u32[]{:S(2)}, u32[]{:S(2)}) %all-to-all-start.8) | async-done | bytes 524320 | tf_op jit(solution)/shard_map/all_to_all | solution.py:341
  159.0 3.6 all-to-all-start.9
  164.5 5.7 %all-to-all-done.9.gy_ref = bf16[8,32,1024]{2,1,0:T(8,128)(2,1)S(1)} async-done(((bf16[8,32,1024]{2,1,0:T(8,128)(2,1)}), bf16[8,32,1024]{2,1,0:T(8,128)(2,1)S(1)}, u32[]{:S(2)}, u32[]{:S(2)}) %all-to-all-start.9) | async-done | bytes 524320 | tf_op jit(solution)/shard_map/all_to_all | solution.py:341
  172.5 10.0 %all-to-all-start.10 = ((bf16[16,144,128]{2,1,0:T(8,128)(2,1)}), bf16[16,144,128]{2,1,0:T(8,128)(2,1)}, u32[]{:S(2)}, u32[]{:S(2)}) async-start(bf16[16,144,128]{2,1,0:T(8,128)(2,1)} %get-tuple-element.121), calls=%async_computation.10 | async-start | bytes 1179648 | tf_op jit(solution)/shard_map/all_to_all | solution.py:341
  189.3 2.9 shard_map.231.gq_ref
  194.4 4.1 shard_map.232
  198.4 3.4 all-to-all-start.11
  205.0 3.3 all-to-all-done.11.parts_ref
  210.0 3.4 all-to-all-start.12
  214.8 4.8 %all-to-all-done.12 = bf16[8,16,1024]{2,1,0:T(8,128)(2,1)S(1)} async-done(((bf16[8,16,1024]{2,1,0:T(8,128)(2,1)}), bf16[8,16,1024]{2,1,0:T(8,128)(2,1)S(1)}, u32[]{:S(2)}, u32[]{:S(2)}) %all-to-all-start.12) | async-done | bytes 262176 | tf_op jit(solution)/shard_map/all_to_all | solution.py:341
  219.6 3.2 shard_map.236
  222.8 3.5 all-to-all-start.13
  231.1 3.4 collective-permute-start.8
  236.2 5.4 %all-to-all-start.14 = ((bf16[8,16,1024]{2,1,0:T(8,128)(2,1)}), bf16[8,16,1024]{2,1,0:T(8,128)(2,1)S(1)}, u32[]{:S(2)}, u32[]{:S(2)}) async-start(bf16[8,16,1024]{2,1,0:T(8,128)(2,1)} %get-tuple-element.143), calls=%async_computation.14 | async-start | bytes 524288 | tf_op jit(solution)/shard_map/all_to_all | solution.py:341
  243.1 5.9 %all-to-all-done.14.gy_ref = bf16[8,16,1024]{2,1,0:T(8,128)(2,1)S(1)} async-done(((bf16[8,16,1024]{2,1,0:T(8,128)(2,1)}), bf16[8,16,1024]{2,1,0:T(8,128)(2,1)S(1)}, u32[]{:S(2)}, u32[]{:S(2)}) %all-to-all-start.14) | async-done | bytes 262176 | tf_op jit(solution)/shard_map/all_to_all | solution.py:341
  251.2 5.1 %all-to-all-start.15 = ((bf16[16,144,128]{2,1,0:T(8,128)(2,1)}), bf16[16,144,128]{2,1,0:T(8,128)(2,1)S(1)}, u32[]{:S(2)}, u32[]{:S(2)}) async-start(bf16[16,144,128]{2,1,0:T(8,128)(2,1)} %get-tuple-element.146), calls=%async_computation.15 | async-start | bytes 1179648 | tf_op jit(solution)/shard_map/all_to_all | solution.py:341
  256.3 2.9 shard_map.239.gq_ref
  265.1 4.1 all-to-all-done.15.got_ref
  269.2 3.9 shard_map.240
  273.1 3.6 all-to-all-start.16
  290.2 4.8 %all-to-all-start.17 = ((bf16[8,24,1024]{2,1,0:T(8,128)(2,1)}), bf16[8,24,1024]{2,1,0:T(8,128)(2,1)S(1)}, u32[]{:S(2)}, u32[]{:S(2)}) async-start(bf16[8,24,1024]{2,1,0:T(8,128)(2,1)} %pad_maximum_fusion.4), calls=%async_computation.17 | async-start | bytes 786432 | tf_op jit(solution)/shard_map/all_to_all | solution.py:341
  298.3 4.7 %all-to-all-done.17 = bf16[8,24,1024]{2,1,0:T(8,128)(2,1)S(1)} async-done(((bf16[8,24,1024]{2,1,0:T(8,128)(2,1)}), bf16[8,24,1024]{2,1,0:T(8,128)(2,1)S(1)}, u32[]{:S(2)}, u32[]{:S(2)}) %all-to-all-start.17) | async-done | bytes 393248 | tf_op jit(solution)/shard_map/all_to_all | solution.py:341
  305.8 6.3 %all-to-all-start.18 = ((bf16[16,8,4224]{2,1,0:T(8,128)(2,1)}), bf16[16,8,4224]{2,1,0:T(8,128)(2,1)S(1)}, u32[]{:S(2)}, u32[]{:S(2)}) async-start(bf16[16,8,4224]{2,1,0:T(8,128)(2,1)} %fusion.1), calls=%async_computation.18 | async-start | bytes 2162688 | tf_op jit(solution)/shard_map/all_to_all | solution.py:341
  312.1 3.0 collective-permute-start.12
  315.2 18.1 %collective-permute-done.12 = bf16[1,32,1024]{2,1,0:T(8,128)(2,1)S(1)} collective-permute-done((bf16[1,32,1024]{2,1,0:T(8,128)(2,1)S(1)}, bf16[1,32,1024]{2,1,0:T(8,128)(2,1)S(1)}, u32[]{:S(2)}, u32[]{:S(2)}) %collective-permute-start.12) | collective-permute-done | bytes 65568 | tf_op jit(solution)/shard_map/ppermute | solution.py:358
  340.8 4.2 collective-permute-done.14
  352.7 4.0 all-to-all-start.19
  358.2 56.3 %all-reduce.4.cloned.1.call-done = (bf16[1,3,1024,128]{3,2,1,0:T(8,128)(2,1)}, bf16[1,128,1024]{2,1,0:T(8,128)(2,1)}, bf16[1,1024,512]{2,1,0:T(8,128)(2,1)}, bf16[1,512,1024]{2,1,0:T(8,128)(2,1)}) async-done(((bf16[1,3,1024,128]{3,2,1,0:T(8,128)(2,1)}, bf16[1,128,1024]{2,1,0:T(8,128)(2,1)}, bf16[1,1024,512]{2,1,0:T(8,128)(2,1)}, bf16[1,512,1024]{2,1,0:T(8,128)(2,1)}), (bf16[1,3,1024,128]{3,2,1,0:T(8,128)(2,1)}, ...) | async-done | bytes 3145744 | tf_op jit(solution)/shard_map/psum | solution.py:631
  414.5 3.6 maximum_convert_fusion
  (208 shorter events, 99.4 us)
Async XLA Ops:
  12.1 36.1 %copy-start.12 = (bf16[2,1024]{1,0:T(2,128)(2,1)S(1)}, bf16[2,1024]{1,0:T(2,128)(2,1)}, u32[]{:S(2)}) copy-start(bf16[2,1024]{1,0:T(2,128)(2,1)} %param.20) | copy-start | bytes 12292
  12.1 26.5 %all-to-all-start = ((bf16[16,128,256]{2,1,0:T(8,128)(2,1)}), bf16[16,128,256]{2,1,0:T(8,128)(2,1)S(1)}, u32[]{:S(2)}, u32[]{:S(2)}) async-start(bf16[16,128,256]{2,1,0:T(8,128)(2,1)} %get-tuple-element.101), calls=%async_computation | async-start | bytes 2097152 | tf_op jit(solution)/shard_map/all_to_all | solution.py:341
  21.4 37.2 %copy-start.18 = (bf16[2,512]{1,0:T(2,128)(2,1)S(1)}, bf16[2,512]{1,0:T(2,128)(2,1)}, u32[]{:S(2)}) copy-start(bf16[2,512]{1,0:T(2,128)(2,1)} %param.22) | copy-start | bytes 6148
  42.2 11.1 %all-to-all-start.1 = ((bf16[8,16,1024]{2,1,0:T(8,128)(2,1)}), bf16[8,16,1024]{2,1,0:T(8,128)(2,1)S(1)}, u32[]{:S(2)}, u32[]{:S(2)}) async-start(bf16[8,16,1024]{2,1,0:T(8,128)(2,1)} %get-tuple-element.102), calls=%async_computation.1 | async-start | bytes 524288 | tf_op jit(solution)/shard_map/all_to_all | solution.py:341
  55.1 9.5 %all-to-all-start.2 = ((bf16[8,16,1024]{2,1,0:T(8,128)(2,1)}), bf16[8,16,1024]{2,1,0:T(8,128)(2,1)S(1)}, u32[]{:S(2)}, u32[]{:S(2)}) async-start(bf16[8,16,1024]{2,1,0:T(8,128)(2,1)} %get-tuple-element.103), calls=%async_computation.2 | async-start | bytes 524288 | tf_op jit(solution)/shard_map/all_to_all | solution.py:341
  67.5 9.5 %all-to-all-start.3 = ((bf16[8,16,1024]{2,1,0:T(8,128)(2,1)}), bf16[8,16,1024]{2,1,0:T(8,128)(2,1)S(1)}, u32[]{:S(2)}, u32[]{:S(2)}) async-start(bf16[8,16,1024]{2,1,0:T(8,128)(2,1)} %get-tuple-element.104), calls=%async_computation.3 | async-start | bytes 524288 | tf_op jit(solution)/shard_map/all_to_all | solution.py:341
  90.9 33.8 %copy-start.8 = (bf16[128,128]{1,0:T(8,128)(2,1)S(1)}, bf16[128,128]{1,0:T(8,128)(2,1)}, u32[]{:S(2)}) copy-start(bf16[128,128]{1,0:T(8,128)(2,1)} %get-tuple-element.100.q_ref) | copy-start | bytes 98308
  90.9 33.8 %copy-start.9 = (bf16[128,128]{1,0:T(8,128)(2,1)S(1)}, bf16[128,128]{1,0:T(8,128)(2,1)}, u32[]{:S(2)}) copy-start(bf16[128,128]{1,0:T(8,128)(2,1)} %get-tuple-element.107.q_ref) | copy-start | bytes 98308
  121.1 9.8 %all-to-all-start.6 = ((bf16[8,16,1024]{2,1,0:T(8,128)(2,1)}), bf16[8,16,1024]{2,1,0:T(8,128)(2,1)S(1)}, u32[]{:S(2)}, u32[]{:S(2)}) async-start(bf16[8,16,1024]{2,1,0:T(8,128)(2,1)} %get-tuple-element.109), calls=%async_computation.6 | async-start | bytes 524288 | tf_op jit(solution)/shard_map/all_to_all | solution.py:341
  124.6 67.6 %all-gather.2.cloned.1.call-start = ((), (), s32[]{:S(2)}) async-start(), calls=%async_computation.20 | async-start | bytes 1114112 | tf_op jit(solution)/shard_map/all_gather | solution.py:479
  146.1 11.0 %all-to-all-start.8 = ((bf16[8,32,1024]{2,1,0:T(8,128)(2,1)}), bf16[8,32,1024]{2,1,0:T(8,128)(2,1)S(1)}, u32[]{:S(2)}, u32[]{:S(2)}) async-start(bf16[8,32,1024]{2,1,0:T(8,128)(2,1)} %get-tuple-element.112), calls=%async_computation.8 | async-start | bytes 1048576 | tf_op jit(solution)/shard_map/all_to_all | solution.py:341
  159.0 30.3 %copy-start.14 = (f32[2,1024]{1,0:T(2,128)S(1)}, f32[2,1024]{1,0:T(2,128)}, u32[]{:S(2)}) copy-start(f32[2,1024]{1,0:T(2,128)} %get-tuple-element.155) | copy-start | bytes 24580
  159.0 11.2 %all-to-all-start.9 = ((bf16[8,32,1024]{2,1,0:T(8,128)(2,1)}), bf16[8,32,1024]{2,1,0:T(8,128)(2,1)S(1)}, u32[]{:S(2)}, u32[]{:S(2)}) async-start(bf16[8,32,1024]{2,1,0:T(8,128)(2,1)} %get-tuple-element.116), calls=%async_computation.9 | async-start | bytes 1048576 | tf_op jit(solution)/shard_map/all_to_all | solution.py:341
  170.2 22.0 %copy-start = (bf16[8,32,1024]{2,1,0:T(8,128)(2,1)}, bf16[8,32,1024]{2,1,0:T(8,128)(2,1)S(1)}, u32[]{:S(2)}) copy-start(bf16[8,32,1024]{2,1,0:T(8,128)(2,1)S(1)} %all-to-all-done.9.gy_ref) | copy-start | bytes 1572868
  172.5 21.8 %all-to-all-start.10 = ((bf16[16,144,128]{2,1,0:T(8,128)(2,1)}), bf16[16,144,128]{2,1,0:T(8,128)(2,1)}, u32[]{:S(2)}, u32[]{:S(2)}) async-start(bf16[16,144,128]{2,1,0:T(8,128)(2,1)} %get-tuple-element.121), calls=%async_computation.10 | async-start | bytes 1179648 | tf_op jit(solution)/shard_map/all_to_all | solution.py:341
  198.4 9.8 %all-to-all-start.11 = ((bf16[8,16,1024]{2,1,0:T(8,128)(2,1)}), bf16[8,16,1024]{2,1,0:T(8,128)(2,1)S(1)}, u32[]{:S(2)}, u32[]{:S(2)}) async-start(bf16[8,16,1024]{2,1,0:T(8,128)(2,1)} %get-tuple-element.124), calls=%async_computation.11 | async-start | bytes 524288 | tf_op jit(solution)/shard_map/all_to_all | solution.py:341
  210.0 9.6 %all-to-all-start.12 = ((bf16[8,16,1024]{2,1,0:T(8,128)(2,1)}), bf16[8,16,1024]{2,1,0:T(8,128)(2,1)S(1)}, u32[]{:S(2)}, u32[]{:S(2)}) async-start(bf16[8,16,1024]{2,1,0:T(8,128)(2,1)} %get-tuple-element.128), calls=%async_computation.12 | async-start | bytes 524288 | tf_op jit(solution)/shard_map/all_to_all | solution.py:341
  222.8 11.7 %copy-start.20 = (f32[1,128]{1,0:T(1,128)S(1)}, f32[1,128]{1,0:T(1,128)}, u32[]{:S(2)}) copy-start(f32[1,128]{1,0:T(1,128)} %get-tuple-element.171) | copy-start | bytes 1540
  222.8 11.7 %copy-start.15 = (f32[2,1024]{1,0:T(2,128)S(1)}, f32[2,1024]{1,0:T(2,128)}, u32[]{:S(2)}) copy-start(f32[2,1024]{1,0:T(2,128)} %get-tuple-element.154) | copy-start | bytes 24580
  222.8 11.7 %all-to-all-start.13 = ((bf16[8,16,1024]{2,1,0:T(8,128)(2,1)}), bf16[8,16,1024]{2,1,0:T(8,128)(2,1)S(1)}, u32[]{:S(2)}, u32[]{:S(2)}) async-start(bf16[8,16,1024]{2,1,0:T(8,128)(2,1)} %get-tuple-element.139), calls=%async_computation.13 | async-start | bytes 524288 | tf_op jit(solution)/shard_map/all_to_all | solution.py:341
  229.1 12.5 %copy-start.5 = (bf16[1024,512]{1,0:T(8,128)(2,1)S(1)}, bf16[1024,512]{1,0:T(8,128)(2,1)}, u32[]{:S(2)}) copy-start(bf16[1024,512]{1,0:T(8,128)(2,1)} %get-tuple-element.175) | copy-start | bytes 3145732
  229.1 13.9 %copy-start.19 = (f32[1,512]{1,0:T(1,128)S(1)}, f32[1,512]{1,0:T(1,128)}, u32[]{:S(2)}) copy-start(f32[1,512]{1,0:T(1,128)} %get-tuple-element.167) | copy-start | bytes 6148
  231.1 28.1 %collective-permute-start.8 = (bf16[8,32,1024]{2,1,0:T(8,128)(2,1)}, bf16[8,32,1024]{2,1,0:T(8,128)(2,1)S(1)}, u32[]{:S(2)}, u32[]{:S(2)}) collective-permute-start(bf16[8,32,1024]{2,1,0:T(8,128)(2,1)} %dynamic-slice_bitcast_fusion), channel_id=1, source_target_pairs={{0,1},{1,0},{2,3},{3,2},{4,5},{5,4},{6,7},{7,6},{8,9},{9,8},{10,11... | collective-permute-start | bytes 1572872 | tf_op jit(solution)/shard_map/ppermute | solution.py:358
  236.2 12.8 %all-to-all-start.14 = ((bf16[8,16,1024]{2,1,0:T(8,128)(2,1)}), bf16[8,16,1024]{2,1,0:T(8,128)(2,1)S(1)}, u32[]{:S(2)}, u32[]{:S(2)}) async-start(bf16[8,16,1024]{2,1,0:T(8,128)(2,1)} %get-tuple-element.143), calls=%async_computation.14 | async-start | bytes 524288 | tf_op jit(solution)/shard_map/all_to_all | solution.py:341
  241.6 172.9 %all-reduce.4.cloned.1.call-start = ((), (), s32[]{:S(2)}) async-start(), calls=%async_computation.21 | async-start | bytes 6291456 | tf_op jit(solution)/shard_map/psum | solution.py:631
  242.5 21.2 %collective-permute-start = (bf16[8,64,512]{2,1,0:T(8,128)(2,1)}, bf16[8,64,512]{2,1,0:T(8,128)(2,1)}, u32[]{:S(2)}, u32[]{:S(2)}) collective-permute-start(bf16[8,64,512]{2,1,0:T(8,128)(2,1)} %dynamic-slice_bitcast_fusion.1), channel_id=1, source_target_pairs={{0,1},{1,0},{2,3},{3,2},{4,5},{5,4},{6,7},{7,6},{8,9},{9,8},{10,11... | collective-permute-start | bytes 1572872 | tf_op jit(solution)/shard_map/ppermute | solution.py:358
  251.2 18.0 %all-to-all-start.15 = ((bf16[16,144,128]{2,1,0:T(8,128)(2,1)}), bf16[16,144,128]{2,1,0:T(8,128)(2,1)S(1)}, u32[]{:S(2)}, u32[]{:S(2)}) async-start(bf16[16,144,128]{2,1,0:T(8,128)(2,1)} %get-tuple-element.146), calls=%async_computation.15 | async-start | bytes 1179648 | tf_op jit(solution)/shard_map/all_to_all | solution.py:341
  261.2 15.6 %collective-permute-start.9 = (bf16[4,32,1024]{2,1,0:T(8,128)(2,1)}, bf16[4,32,1024]{2,1,0:T(8,128)(2,1)}, u32[]{:S(2)}, u32[]{:S(2)}) collective-permute-start(bf16[4,32,1024]{2,1,0:T(8,128)(2,1)} %dynamic-slice_bitcast_fusion.2), channel_id=1, source_target_pairs={{0,12},{1,13},{2,14},{3,15},{4,8},{5,9},{6,10},{7,11},{8,4},{9,5},... | collective-permute-start | bytes 786440 | tf_op jit(solution)/shard_map/ppermute | solution.py:358
  265.0 19.6 %collective-permute-start.1 = (bf16[4,64,512]{2,1,0:T(8,128)(2,1)S(1)}, bf16[4,64,512]{2,1,0:T(8,128)(2,1)S(1)}, u32[]{:S(2)}, u32[]{:S(2)}) collective-permute-start(bf16[4,64,512]{2,1,0:T(8,128)(2,1)S(1)} %dynamic-slice_bitcast_fusion.3), channel_id=1, source_target_pairs={{0,4},{1,5},{2,6},{3,7},{4,0},{5,1},{6,2},{7,3},{8,12},{9,13},{10,... | collective-permute-start | bytes 786440 | tf_op jit(solution)/shard_map/ppermute | solution.py:358
  273.1 12.1 %all-to-all-start.16 = ((bf16[8,16,1024]{2,1,0:T(8,128)(2,1)}), bf16[8,16,1024]{2,1,0:T(8,128)(2,1)S(1)}, u32[]{:S(2)}, u32[]{:S(2)}) async-start(bf16[8,16,1024]{2,1,0:T(8,128)(2,1)} %get-tuple-element.149), calls=%async_computation.16 | async-start | bytes 524288 | tf_op jit(solution)/shard_map/all_to_all | solution.py:341
  282.5 12.6 %collective-permute-start.10 = (bf16[2,32,1024]{2,1,0:T(8,128)(2,1)S(1)}, bf16[2,32,1024]{2,1,0:T(8,128)(2,1)S(1)}, u32[]{:S(2)}, u32[]{:S(2)}) collective-permute-start(bf16[2,32,1024]{2,1,0:T(8,128)(2,1)S(1)} %dynamic-slice_bitcast_fusion.4), channel_id=1, source_target_pairs={{0,4},{1,5},{2,6},{3,7},{4,0},{5,1},{6,2},{7,3},{8,12},{9,13},{10,... | collective-permute-start | bytes 393224 | tf_op jit(solution)/shard_map/ppermute | solution.py:358
  284.6 20.1 %copy-start.10 = (bf16[128,1024]{1,0:T(8,128)(2,1)S(1)}, bf16[128,1024]{1,0:T(8,128)(2,1)}, u32[]{:S(2)}) copy-start(bf16[128,1024]{1,0:T(8,128)(2,1)} %get-tuple-element.159) | copy-start | bytes 786436
  284.7 12.0 %collective-permute-start.2 = (bf16[2,64,512]{2,1,0:T(8,128)(2,1)S(1)}, bf16[2,64,512]{2,1,0:T(8,128)(2,1)S(1)}, u32[]{:S(2)}, u32[]{:S(2)}) collective-permute-start(bf16[2,64,512]{2,1,0:T(8,128)(2,1)S(1)} %dynamic-slice_bitcast_fusion.5), channel_id=1, source_target_pairs={{0,12},{1,13},{2,14},{3,15},{4,8},{5,9},{6,10},{7,11},{8,4},{9,5},... | collective-permute-start | bytes 393224 | tf_op jit(solution)/shard_map/ppermute | solution.py:358
  290.2 12.8 %all-to-all-start.17 = ((bf16[8,24,1024]{2,1,0:T(8,128)(2,1)}), bf16[8,24,1024]{2,1,0:T(8,128)(2,1)S(1)}, u32[]{:S(2)}, u32[]{:S(2)}) async-start(bf16[8,24,1024]{2,1,0:T(8,128)(2,1)} %pad_maximum_fusion.4), calls=%async_computation.17 | async-start | bytes 786432 | tf_op jit(solution)/shard_map/all_to_all | solution.py:341
  295.1 17.0 %collective-permute-start.11 = (bf16[1,32,1024]{2,1,0:T(8,128)(2,1)S(1)}, bf16[1,32,1024]{2,1,0:T(8,128)(2,1)S(1)}, u32[]{:S(2)}, u32[]{:S(2)}) collective-permute-start(bf16[1,32,1024]{2,1,0:T(8,128)(2,1)S(1)} %constant_dynamic-slice_fusion), channel_id=1, source_target_pairs={{0,2},{1,3},{2,0},{3,1},{4,6},{5,7},{6,4},{7,5},{8,10},{9,11},{10,... | collective-permute-start | bytes 196616 | tf_op jit(solution)/shard_map/ppermute | solution.py:358
  296.7 18.4 %collective-permute-start.3 = (bf16[1,64,512]{2,1,0:T(8,128)(2,1)S(1)}, bf16[1,64,512]{2,1,0:T(8,128)(2,1)S(1)}, u32[]{:S(2)}, u32[]{:S(2)}) collective-permute-start(bf16[1,64,512]{2,1,0:T(8,128)(2,1)S(1)} %constant_dynamic-slice_fusion.1), channel_id=1, source_target_pairs={{0,2},{1,3},{2,0},{3,1},{4,6},{5,7},{6,4},{7,5},{8,10},{9,11},{10,... | collective-permute-start | bytes 196616 | tf_op jit(solution)/shard_map/ppermute | solution.py:358
  303.0 12.3 %copy-start.4 = (bf16[8,24,1024]{2,1,0:T(8,128)(2,1)}, bf16[8,24,1024]{2,1,0:T(8,128)(2,1)S(1)}, u32[]{:S(2)}) copy-start(bf16[8,24,1024]{2,1,0:T(8,128)(2,1)S(1)} %all-to-all-done.17) | copy-start | bytes 1179652
  305.8 45.8 %all-to-all-start.18 = ((bf16[16,8,4224]{2,1,0:T(8,128)(2,1)}), bf16[16,8,4224]{2,1,0:T(8,128)(2,1)S(1)}, u32[]{:S(2)}, u32[]{:S(2)}) async-start(bf16[16,8,4224]{2,1,0:T(8,128)(2,1)} %fusion.1), calls=%async_computation.18 | async-start | bytes 2162688 | tf_op jit(solution)/shard_map/all_to_all | solution.py:341
  312.1 21.3 %collective-permute-start.12 = (bf16[1,32,1024]{2,1,0:T(8,128)(2,1)S(1)}, bf16[1,32,1024]{2,1,0:T(8,128)(2,1)S(1)}, u32[]{:S(2)}, u32[]{:S(2)}) collective-permute-start(bf16[1,32,1024]{2,1,0:T(8,128)(2,1)S(1)} %add_convert_fusion), channel_id=1, source_target_pairs={{0,2},{1,3},{2,0},{3,1},{4,6},{5,7},{6,4},{7,5},{8,10},{9,11},{10,... | collective-permute-start | bytes 196616 | tf_op jit(solution)/shard_map/ppermute | solution.py:358
  315.1 19.9 %collective-permute-start.4 = (bf16[1,64,512]{2,1,0:T(8,128)(2,1)S(1)}, bf16[1,64,512]{2,1,0:T(8,128)(2,1)S(1)}, u32[]{:S(2)}, u32[]{:S(2)}) collective-permute-start(bf16[1,64,512]{2,1,0:T(8,128)(2,1)S(1)} %add_convert_fusion.1), channel_id=1, source_target_pairs={{0,2},{1,3},{2,0},{3,1},{4,6},{5,7},{6,4},{7,5},{8,10},{9,11},{10,... | collective-permute-start | bytes 196616 | tf_op jit(solution)/shard_map/ppermute | solution.py:358
  333.4 3.9 collective-permute-start.13
  335.0 5.7 %collective-permute-start.5 = (bf16[2,64,512]{2,1,0:T(8,128)(2,1)S(1)}, bf16[2,64,512]{2,1,0:T(8,128)(2,1)S(1)}, u32[]{:S(2)}, u32[]{:S(2)}) collective-permute-start(bf16[2,64,512]{2,1,0:T(8,128)(2,1)S(1)} %pad_maximum_fusion.7), channel_id=1, source_target_pairs={{0,12},{1,13},{2,14},{3,15},{4,8},{5,9},{6,10},{7,11},{8,4},{9,5},... | collective-permute-start | bytes 393224 | tf_op jit(solution)/shard_map/ppermute | solution.py:358
  337.4 7.7 %collective-permute-start.14 = (bf16[4,32,1024]{2,1,0:T(8,128)(2,1)S(1)}, bf16[4,32,1024]{2,1,0:T(8,128)(2,1)S(1)}, u32[]{:S(2)}, u32[]{:S(2)}) collective-permute-start(bf16[4,32,1024]{2,1,0:T(8,128)(2,1)S(1)} %pad_maximum_fusion.6), channel_id=1, source_target_pairs={{0,12},{1,13},{2,14},{3,15},{4,8},{5,9},{6,10},{7,11},{8,4},{9,5},... | collective-permute-start | bytes 786440 | tf_op jit(solution)/shard_map/ppermute | solution.py:358
  340.7 9.9 %slice-start.1 = ((bf16[8,24,1024]{2,1,0:T(8,128)(2,1)}), bf16[8,16,1024]{2,1,0:T(8,128)(2,1)S(1)}, s32[]{:S(2)}) async-start(bf16[8,24,1024]{2,1,0:T(8,128)(2,1)} %copy-done.4), calls=%async_computation.23 | async-start | bytes 524288 | tf_op jit(solution)/shard_map/slice | solution.py:634
  340.7 8.0 %collective-permute-start.6 = (bf16[4,64,512]{2,1,0:T(8,128)(2,1)S(1)}, bf16[4,64,512]{2,1,0:T(8,128)(2,1)S(1)}, u32[]{:S(2)}, u32[]{:S(2)}) collective-permute-start(bf16[4,64,512]{2,1,0:T(8,128)(2,1)S(1)} %pad_maximum_fusion.5), channel_id=1, source_target_pairs={{0,4},{1,5},{2,6},{3,7},{4,0},{5,1},{6,2},{7,3},{8,12},{9,13},{10,... | collective-permute-start | bytes 786440 | tf_op jit(solution)/shard_map/ppermute | solution.py:358
  346.0 10.8 %collective-permute-start.15 = (bf16[8,32,1024]{2,1,0:T(8,128)(2,1)}, bf16[8,32,1024]{2,1,0:T(8,128)(2,1)S(1)}, u32[]{:S(2)}, u32[]{:S(2)}) collective-permute-start(bf16[8,32,1024]{2,1,0:T(8,128)(2,1)} %pad_maximum_fusion.3), channel_id=1, source_target_pairs={{0,1},{1,0},{2,3},{3,2},{4,5},{5,4},{6,7},{7,6},{8,9},{9,8},{10,11... | collective-permute-start | bytes 1572872 | tf_op jit(solution)/shard_map/ppermute | solution.py:358
  349.6 7.3 %collective-permute-start.7 = (bf16[8,64,512]{2,1,0:T(8,128)(2,1)}, bf16[8,64,512]{2,1,0:T(8,128)(2,1)}, u32[]{:S(2)}, u32[]{:S(2)}) collective-permute-start(bf16[8,64,512]{2,1,0:T(8,128)(2,1)} %pad_maximum_fusion.2), channel_id=1, source_target_pairs={{0,1},{1,0},{2,3},{3,2},{4,5},{5,4},{6,7},{7,6},{8,9},{9,8},{10,11... | collective-permute-start | bytes 1572872 | tf_op jit(solution)/shard_map/ppermute | solution.py:358
  352.7 67.6 %all-to-all-start.19 = ((bf16[16,8,4224]{2,1,0:T(8,128)(2,1)}), bf16[16,8,4224]{2,1,0:T(8,128)(2,1)S(1)}, u32[]{:S(2)}, u32[]{:S(2)}) async-start(bf16[16,8,4224]{2,1,0:T(8,128)(2,1)} %broadcast_in_dim.15), calls=%async_computation.19 | async-start | bytes 2162688 | tf_op jit(solution)/shard_map/all_to_all | solution.py:341
  (12 other events, 52.1 us)
Sparse Core Ops, SparseCore 0:
  127.8 44.9 all-gather.1
  245.8 168.6 all-reduce.3
